TPU v7x, 32 devices: a whole 2x2x4 slice. The times are simulated.
32 devices in a mesh: subj: 4 (over x, core), space: 8 (over z, y).
Axes of the slice: x: 2, y: 2, z: 4, core: 2. Of those that a mesh axis runs over, the one named last changes fastest.
Arguments:
- images: bfloat16 [8, 512, 16, 128], P('subj', 'space'), may hold values from -6 to 6
- velocity: float32 [3, 8, 512, 16, 128], P(None, 'subj', 'space'), may hold values from -4 to 4
- weights: bfloat16 [3, 8, 512, 16, 128], P(None, 'subj', 'space'), may hold values from 0 to 1
- template: float32 [512, 16, 128], P('space', 'subj'), may hold values from -6 to 6
- owners: int32 [8, 512, 1], P('subj', 'space'), may hold values from 0 to 7; in each aligned block of 64 rows (0 to 63, 64 to 127, ..., all dimensions but the last counted through in order) at most 16 rows name the same one
- local_rows: int32 [8, 512], P('subj', 'space'), may hold values from 0 to 63
- tile_counts: int32 [8, 8], P('subj', 'space'), may hold values from 32 to 64
Outputs:
- new_velocity: float32 [3, 8, 512, 16, 128], P(None, 'subj', 'space')
- new_template: float32 [512, 16, 128], P('space', 'subj')
Inputs may be any that keep to these rules, and one draw needn't show every extreme that they name: `owners`: for each subject and each aligned block of 64 tiles, no value appears more than 16 times, and some value appears exactly 16 times.
All inputs are finite; a program needn't handle non-finite values.
Results may differ from a plain program's by a relative error of at most 0.0006.
Values may be sent and summed in bfloat16 or wider, within the bound.
No kernel may reach another device: no remote copies, remote signals or barrier semaphores. Data moves between devices by JAX's collectives and lax.ppermute only.
A program may use at most 64 MiB of HBM per device.

v0:
```python
import functools

import jax
import jax.numpy as jnp
from jax import lax
from jax.experimental import pallas as pl
from jax.experimental.pallas import tpu as pltpu
from jax.sharding import PartitionSpec as P

BY = 4
ITERS = 2
RIDGE = 0.25
LANES = 128
LIMIT = 24 * 1024 * 1024
EDGE = 2
CODES = 48
HEAD = 8
COUNTS = 64
SHIFT = 8

VMEM = pl.BlockSpec(memory_space=pltpu.VMEM)
SMEM = pl.BlockSpec(memory_space=pltpu.SMEM)
ANY = pl.BlockSpec(memory_space=pl.ANY)
SMALL = pl.CostEstimate(flops=0, bytes_accessed=0, transcendentals=0)


def params():
    return pltpu.CompilerParams(vmem_limit_bytes=LIMIT)


def shaped(shape, dtype=jnp.float32):
    return jax.ShapeDtypeStruct(shape, dtype)


def in_hbm(value):
    return pltpu.with_memory_space_constraint(value, pltpu.HBM)


def in_vmem(value):
    return pltpu.with_memory_space_constraint(value, pltpu.VMEM)


def plan_kernel(
    cap,
    counts_in,
    owners_in,
    rows_in,
    images_ref,
    template_ref,
    request_ref,
    slots_ref,
    held_ref,
    counts_ref,
    owners_ref,
    rows_ref,
    ends_ref,
    sems,
):
    subj_dev, rows = rows_ref.shape
    spaces = request_ref.shape[0]
    share = template_ref.shape[1]
    me = lax.axis_index("space")
    copies = [
        pltpu.make_async_copy(source, target, sems.at[i])
        for i, (source, target) in enumerate(
            (
                (counts_in, counts_ref),
                (owners_in, owners_ref),
                (rows_in, rows_ref),
                (template_ref.at[pl.ds(0, EDGE)], ends_ref.at[0]),
                (template_ref.at[pl.ds(rows - EDGE, EDGE)], ends_ref.at[1]),
                (images_ref, held_ref),
            )
        )
    ]
    for copy in copies:
        copy.start()
    for copy in copies[:3]:
        copy.wait()
    t = lax.broadcasted_iota(jnp.int32, (rows, rows), 0)
    u = lax.broadcasted_iota(jnp.int32, (rows, rows), 1)
    eye = t == u
    lane = lax.broadcasted_iota(jnp.int32, (rows, LANES), 1)
    line = lax.broadcasted_iota(jnp.int32, (1, LANES), 1)
    sub = lax.broadcasted_iota(jnp.int32, (spaces, LANES), 0)
    zero = jnp.zeros((rows, rows), jnp.int32)
    request = jnp.zeros((spaces, LANES), jnp.int32)
    extra = jnp.zeros((1, LANES), jnp.int32)
    earlier_subjects = []
    for s in range(subj_dev):
        count = counts_ref[0, s]
        first = lax.shift_right_logical(count, 1)
        owner_u = jnp.broadcast_to(owners_ref[s], (rows, rows))
        row_u = jnp.broadcast_to(rows_ref[s : s + 1, :], (rows, rows))
        owner_t = jnp.broadcast_to(
            jnp.sum(jnp.where(eye, owner_u, zero), axis=1, keepdims=True), (rows, rows)
        )
        row_t = jnp.broadcast_to(
            jnp.sum(jnp.where(eye, row_u, zero), axis=1, keepdims=True), (rows, rows)
        )
        last = rows - (count - first)
        alive_t = (t < first) | (t >= last)
        alive_u = (u < first) | (u >= last)
        same_owner = owner_t == owner_u
        same = same_owner & (row_t == row_u)
        dup_u = jnp.sum(jnp.where(same & alive_t & (t < u), 1, 0), axis=0, keepdims=True)
        dup_t = jnp.sum(jnp.where(same & alive_u & (u < t), 1, 0), axis=1, keepdims=True)
        first_u = alive_u & jnp.broadcast_to(dup_u == 0, (rows, rows))
        first_t = alive_t & jnp.broadcast_to(dup_t == 0, (rows, rows))
        place = jnp.sum(jnp.where(same_owner & first_u & (u < t), 1, 0), axis=1, keepdims=True)
        for owner_v, first_v in earlier_subjects:
            place = place + jnp.sum(
                jnp.where((owner_t == owner_v) & first_v, 1, 0), axis=1, keepdims=True
            )
        earlier_subjects.append((owner_u, first_u))
        slot_t = owner_t * cap + place
        slots_ref[s : s + 1, :] = jnp.sum(
            jnp.where(same & first_t & alive_u, slot_t, zero), axis=0, keepdims=True
        )
        wide_first = jnp.broadcast_to(first_t[:, :1], (rows, LANES))
        wide_owner = jnp.broadcast_to(owner_t[:, :1], (rows, LANES))
        wide_place = jnp.broadcast_to(place, (rows, LANES))
        wide_row = jnp.broadcast_to(row_t[:, :1], (rows, LANES)) + s * rows
        wide_tile = lax.broadcasted_iota(jnp.int32, (rows, LANES), 0)
        hit = jnp.where(wide_first & (wide_place == lane), wide_row, 0)
        for o in range(spaces):
            asked = jnp.sum(jnp.where(wide_owner == o, hit, 0), axis=0, keepdims=True)
            request = request + jnp.where(sub == o, asked, 0)
        counted = jnp.where(wide_first & (wide_owner == lane - COUNTS), 1, 0)
        extra = extra + jnp.sum(counted, axis=0, keepdims=True)
        for side, begin in enumerate((0, rows - EDGE)):
            place = CODES + (side * subj_dev + s) * EDGE
            code = jnp.where(
                wide_tile - begin == lane - place, lax.shift_left(wide_owner, SHIFT) + wide_row, 0
            )
            code = jnp.sum(code, axis=0, keepdims=True)
            extra = extra + jnp.where((line >= place) & (line < place + EDGE), code, 0)
    request = (request + jnp.broadcast_to(extra, request.shape)).astype(jnp.float32)
    for copy in copies[3:]:
        copy.wait()
    for o in range(spaces):
        request_ref[o, :HEAD] = jnp.broadcast_to(request[o : o + 1], (HEAD, LANES))
        for r in range(EDGE):
            at = HEAD + r * share
            request_ref[o, at : at + share] = jnp.where(o < me, ends_ref[0, r], ends_ref[1, r])
        if HEAD + EDGE * share < request_ref.shape[1]:
            rest = request_ref.shape[1] - HEAD - EDGE * share
            request_ref[o, HEAD + EDGE * share :] = jnp.zeros((rest, LANES), jnp.float32)


def plan(counts, owners, local_rows, images, template, cap, spaces):
    subj_dev, rows = local_rows.shape
    share = template.shape[1]
    lines = HEAD + -(-EDGE * share // 8) * 8
    return pl.pallas_call(
        functools.partial(plan_kernel, cap),
        out_shape=(
            shaped((spaces, lines, LANES)),
            shaped((subj_dev, rows), jnp.int32),
            pltpu.VMEM(images.shape, images.dtype),
        ),
        in_specs=[ANY] * 5,
        out_specs=(VMEM, VMEM, VMEM),
        scratch_shapes=[
            pltpu.SMEM(counts.shape, jnp.int32),
            pltpu.VMEM(owners.shape, jnp.int32),
            pltpu.VMEM(local_rows.shape, jnp.int32),
            pltpu.VMEM((2, EDGE, share, LANES), jnp.float32),
            pltpu.SemaphoreType.DMA((6,)),
        ],
        compiler_params=params(),
        name="plan",
    )(*map(in_hbm, (counts, owners, local_rows, images, template)))


def edge_codes(wanted_ref, me, subj_dev):
    spaces = wanted_ref.shape[0]
    before, after = jnp.maximum(me - 1, 0), jnp.minimum(me + 1, spaces - 1)
    found = []
    for i in range(subj_dev * EDGE):
        found.append((wanted_ref[before, CODES + subj_dev * EDGE + i], me > 0))
    for i in range(subj_dev * EDGE):
        found.append((wanted_ref[after, CODES + i], me < spaces - 1))
    return found


def crowded(wanted, base, size, subj_dev):
    spaces, lanes = wanted.shape
    d = lax.broadcasted_iota(jnp.int32, (spaces, lanes), 0)
    owner = lax.broadcasted_iota(jnp.int32, (spaces, lanes), 1) - COUNTS
    need = wanted
    for side in range(2):
        codes = pltpu.roll(wanted, 1 if side == 0 else spaces - 1, 0)
        valid = d > 0 if side == 0 else d < spaces - 1
        begin = CODES + (subj_dev * EDGE if side == 0 else 0)
        for i in range(subj_dev * EDGE):
            code = jnp.broadcast_to(codes[:, begin + i : begin + i + 1], (spaces, lanes))
            hit = valid & (lax.shift_right_logical(code, SHIFT) == owner)
            need = need + jnp.where(hit, 1, 0)
    pair = (owner >= 0) & (owner < spaces) & (lax.bitwise_xor(owner, d) >= base)
    over = jnp.where(pair & (need > size), 1.0, 0.0)
    return jnp.max(jnp.max(over, axis=0, keepdims=True), axis=1, keepdims=True)


def pick_kernel(cap, base, total, answers_ref, images_ref, template_ref, velocity_ref, weights_ref, *refs):
    spaces = answers_ref.shape[0]
    sends, overs = refs[:spaces], refs[spaces : 2 * spaces - base]
    edge_slots, side_ref, ends_ref, requests_ref, wanted_ref, used, v_ref, w_ref, sems = refs[-9:]
    rows, share = template_ref.shape[:2]
    subj_dev = velocity_ref.shape[1]
    me = lax.axis_index("space")
    odd = lax.bitwise_and(me, 1)
    fetches = [pltpu.make_async_copy(template_ref, ends_ref.at[pl.ds(0, rows)], sems.at[0])]
    for side, begin in enumerate((0, rows - EDGE)):
        part = pl.ds(begin, EDGE)
        place = lax.bitwise_xor(odd, 1 - side)
        for i, (source, target) in enumerate(((velocity_ref, v_ref), (weights_ref, w_ref))):
            fetches.append(
                pltpu.make_async_copy(
                    source.at[:, :, part], target.at[place], sems.at[2 + 2 * side + i]
                )
            )
    for copy in fetches:
        copy.start()
    for d in range(spaces):
        requests_ref[d : d + 1] = answers_ref[d, :1].astype(jnp.int32)
    move = pltpu.make_async_copy(requests_ref, wanted_ref, sems.at[1])
    move.start()
    for side, neighbour in enumerate((jnp.maximum(me - 1, 0), jnp.minimum(me + 1, spaces - 1))):
        for r in range(EDGE):
            at = HEAD + r * share
            ends_ref[rows + side * EDGE + r] = answers_ref[neighbour, at : at + share]
    move.wait()
    for k in range(spaces):
        target = lax.bitwise_xor(me, k)
        size = sends[k].shape[0] if k >= base else total

        def put(c, brick, k=k, size=size):
            if isinstance(c, int):
                ref, c = (sends[k], c) if c < size else (overs[k - base], c - size)
                ref[c] = brick
            elif k < base:
                sends[k][c] = brick
            else:

                @pl.when(c < size)
                def _():
                    sends[k][c] = brick

                @pl.when(c >= size)
                def _():
                    overs[k - base][c - size] = brick

        for c in range(cap):
            put(c, images_ref[wanted_ref[target, c]])
        place = wanted_ref[target, COUNTS + me]
        for code, valid in edge_codes(wanted_ref, target, subj_dev):
            mine = valid & (lax.shift_right_logical(code, SHIFT) == me)

            @pl.when(mine)
            def _(code=code, place=place, put=put):
                put(place, images_ref[lax.bitwise_and(code, (1 << SHIFT) - 1)])

            place = place + jnp.where(mine, 1, 0)
    ends_ref[rows + 2 * EDGE] = jnp.broadcast_to(
        crowded(requests_ref[...], base, sends[-1].shape[0], subj_dev), ends_ref.shape[1:]
    )
    for o in range(spaces):
        used[o] = wanted_ref[me, COUNTS + o]
    for i, (code, valid) in enumerate(edge_codes(wanted_ref, me, subj_dev)):
        owner = jnp.where(valid, lax.shift_right_logical(code, SHIFT), 0)
        place = used[owner]
        edge_slots[i] = jnp.where(valid, lax.bitwise_xor(owner, me) * total + place, 0)
        used[owner] = place + jnp.where(valid, 1, 0)
    for copy in fetches:
        copy.wait()
    for side, (out, i) in enumerate(((sends[1], total), (side_ref, 0))):
        for c in range(3):
            for s in range(subj_dev):
                for r in range(EDGE):
                    out[i] = v_ref[side, c, s, r].astype(out.dtype)
                    out[i + 1] = w_ref[side, c, s, r]
                    i = i + 2


def pick(answers, images, template, velocity, weights, cap, sizes):
    spaces = answers.shape[0]
    subj_dev = velocity.shape[1]
    total = cap + 2 * EDGE * subj_dev
    tile = images.shape[1:]
    packed = 2 * EDGE * 3 * subj_dev
    base = sizes.index(min(sizes))
    longer = [n + packed if k == 1 else n for k, n in enumerate(sizes)]
    outs = [shaped((n,) + tile, images.dtype) for n in longer]
    outs += [shaped((total - n,) + tile, images.dtype) for n in sizes[base:]]
    got = pl.pallas_call(
        functools.partial(pick_kernel, cap, base, total),
        out_shape=outs
        + [
            shaped((2 * EDGE * subj_dev,), jnp.int32),
            shaped((packed,) + tile, images.dtype),
            shaped((template.shape[0] + 2 * EDGE + 1,) + template.shape[1:]),
        ],
        in_specs=[VMEM, VMEM, ANY, ANY, ANY],
        out_specs=[VMEM] * len(outs) + [SMEM, VMEM, VMEM],
        scratch_shapes=[
            pltpu.VMEM((spaces, LANES), jnp.int32),
            pltpu.SMEM((spaces, LANES), jnp.int32),
            pltpu.SMEM((spaces,), jnp.int32),
            pltpu.VMEM((2, 3, subj_dev, EDGE) + tile, velocity.dtype),
            pltpu.VMEM((2, 3, subj_dev, EDGE) + tile, weights.dtype),
            pltpu.SemaphoreType.DMA((6,)),
        ],
        compiler_params=params(),
        name="pick",
    )(answers, images, *map(in_hbm, (template, velocity, weights)))
    return got[:spaces], got[spaces:-3], *got[-3:]


def up_x(v):
    return pltpu.roll(v, v.shape[0] - BY, 0)


def up_y(v):
    return pltpu.roll(v, v.shape[0] - 1, 0)


def up_z(v):
    return pltpu.roll(v, v.shape[1] - 1, 1)


def down_x(v):
    return pltpu.roll(v, BY, 0)


def down_y(v):
    return pltpu.roll(v, 1, 0)


def down_z(v):
    return pltpu.roll(v, 1, 1)


def inside(shape, value):
    p = lax.broadcasted_iota(jnp.int32, shape, 0)
    z = lax.broadcasted_iota(jnp.int32, shape, 1)
    y = lax.bitwise_and(p, BY - 1)
    conditions = (
        p < shape[0] - BY,
        p >= BY,
        y < BY - 1,
        y > 0,
        z < shape[1] - 1,
        z > 0,
    )
    return [jnp.where(c, value, 0.0).astype(jnp.float32) for c in conditions]


def warp_tile(brick, fractions, masks, live):
    frac_x, frac_y, frac_z = (f.astype(jnp.float32) for f in fractions)
    high_x, high_y, high_z = frac_x * masks[0], frac_y * masks[2], frac_z * masks[4]
    low_x, low_y, low_z = 1.0 - frac_x, 1.0 - frac_y, 1.0 - frac_z
    low_x, high_x = low_x * live, high_x * live

    def along_z(v):
        return low_z * v + high_z * up_z(v)

    def along_y(v):
        return low_y * along_z(v) + high_y * along_z(up_y(v))

    return low_x * along_y(brick) + high_x * along_y(up_x(brick))


def slopes(w, halves):
    return (
        up_x(w) * halves[0] - down_x(w) * halves[1],
        up_y(w) * halves[2] - down_y(w) * halves[3],
        up_z(w) * halves[4] - down_z(w) * halves[5],
    )


def predict(w, g, f):
    return w + (g[0] * f[0] + g[1] * f[1]) + g[2] * f[2]


def smooth(before, here, after, masks):
    rowwise = (before + after) + (here + here)
    return (down_z(rowwise) * masks[5] + up_z(rowwise) * masks[4]) + (rowwise + rowwise)


def first_kernel(spaces, base, groups, *refs):
    counts_ref, slots_ref, edge_slots_ref = refs[:3]
    parts, refs = refs[3 : 3 + spaces], refs[3 + spaces :]
    overs, refs = refs[: spaces - base], refs[spaces - base :]
    shares, refs = refs[:groups], refs[groups:]
    side_ref, weights_in, velocity_in = refs[:3]
    warped_ref, slopes_ref, scale_ref, field_ref, keep_ref, send_ref = refs[3:9]
    table, update, weights_ref, packs, chunk_sems = refs[9:]
    _, subj_dev, rows, plane, depth = weights_ref.shape
    total = parts[0].shape[0]
    short = parts[-1].shape[0]
    cap = total - 2 * EDGE * subj_dev
    me, position = lax.axis_index("space"), lax.axis_index("subj")
    core = lax.bitwise_and(position, 1)
    odd = lax.bitwise_and(me, 1)
    chunks = chunk_sems.shape[0] // 2
    chunk = rows // chunks
    chunk_copies = []
    for i in range(chunks):
        part = pl.ds(i * chunk, chunk)
        chunk_copies.append(
            [
                pltpu.make_async_copy(source.at[:, :, part], target, chunk_sems.at[n])
                for n, source, target in (
                    (2 * i, weights_in, weights_ref.at[:, :, part]),
                    (2 * i + 1, velocity_in, field_ref.at[:, :, pl.ds(1 + i * chunk, chunk)]),
                )
            ]
        )
    for copy in sum(chunk_copies, []):
        copy.start()
    for k in range(spaces):
        for c in range(total):
            if k < base or c < short:
                table[k * total + c] = parts[k][c]
            else:
                table[k * total + c] = overs[k - base][c - short]
    for i in range(packs.shape[1]):
        packs[1 - odd, i] = parts[1][total + i]
        packs[odd, i] = side_ref[i]
    before_ref, after_ref = packs.at[0], packs.at[1]
    masks, halves = inside((plane, depth), 1.0), inside((plane, depth), 0.5)

    def tile(s, e, brick, fractions, live, f, current):
        w = warp_tile(brick.astype(jnp.float32), fractions, masks, live)
        g = slopes(w, halves)
        scale = 0.0625 / (g[0] * g[0] + g[1] * g[1] + g[2] * g[2] + RIDGE)
        ratio = (predict(w, g, f) - current) * scale
        warped_ref[s, e] = w
        scale_ref[s, e] = scale
        for c in range(3):
            slopes_ref[c, s, e] = g[c]
            update[c, s, e] = g[c] * ratio

    def template_row(r):
        parts = [shares[k][r] for k in range(groups)]
        mask = 1
        while mask < groups:
            turned = lax.bitwise_and(position, mask) > 0
            parts = [jnp.where(turned, parts[i ^ mask], part) for i, part in enumerate(parts)]
            mask = 2 * mask
        return jnp.concatenate(parts, axis=0)

    def row(r, carry):
        current = template_row(r)
        for s in range(subj_dev):
            count = counts_ref[0, s]
            first = lax.shift_right_logical(count, 1)
            alive = (r < first) | (r >= rows - (count - first))
            live = jnp.where(alive, 1.0, 0.0).astype(jnp.float32)
            wanted = slots_ref[s, r]
            owner = lax.div(wanted, cap)
            slot = lax.bitwise_xor(owner, me) * total + (wanted - owner * cap)
            tile(
                s,
                r + EDGE,
                table[slot],
                [weights_ref[c, s, r] for c in range(3)],
                live,
                [field_ref[c, s, r + 1] for c in range(3)],
                current,
            )
        return carry

    for side, (ref, there, e0) in enumerate(
        ((before_ref, me > 0, 0), (after_ref, me < spaces - 1, rows + EDGE))
    ):
        live = jnp.where(there, 1.0, 0.0).astype(jnp.float32)
        for r in range(EDGE):
            current = template_row(rows + side * EDGE + r)
            for s in range(subj_dev):
                at = [2 * ((c * subj_dev + s) * EDGE + r) for c in range(3)]
                tile(
                    s,
                    e0 + r,
                    table[edge_slots_ref[(side * subj_dev + s) * EDGE + r]],
                    [ref[a + 1] for a in at],
                    live,
                    [ref[a].astype(jnp.float32) for a in at],
                    current,
                )

    for i in range(chunks):
        for copy in chunk_copies[i]:
            copy.wait()
        lax.fori_loop(i * chunk, (i + 1) * chunk, row, 0, unroll=8)

    for c in range(3):
        for s in range(subj_dev):
            at = 2 * (c * subj_dev + s) * EDGE
            field_ref[c, s, 0] = before_ref[at + 2 * (EDGE - 1)].astype(jnp.float32)
            field_ref[c, s, rows + 1] = after_ref[at].astype(jnp.float32)

    def move(i, carry):
        e = i + EDGE - 1
        total_p = None
        for s in range(subj_dev):
            g = [slopes_ref[c, s, e] for c in range(3)]
            f = []
            for c in range(3):
                delta = smooth(update[c, s, e - 1], update[c, s, e], update[c, s, e + 1], masks)
                f.append(field_ref[c, s, i] - delta)
                field_ref[c, s, i] = f[c]
            p = predict(warped_ref[s, e], g, f)
            total_p = p if total_p is None else total_p + p
        half = plane // 2
        low, high = total_p[:half], total_p[half:]
        keep_ref[i] = jnp.where(core == 0, low, high)
        send_ref[i] = jnp.where(core == 0, high, low)
        return carry

    lax.fori_loop(0, rows + 2, move, 0, unroll=11)


def first(counts, slots, edge_slots, parts, overs, shares, side, weights, velocity):
    _, subj_dev, rows, plane, depth = velocity.shape
    spaces = len(parts)
    total = parts[0].shape[0]
    long = rows + 2 * EDGE
    sums = shaped((rows + 2, plane // 2, depth))
    arrays = [*parts, *overs, *shares, side]
    return pl.pallas_call(
        functools.partial(first_kernel, spaces, spaces - len(overs), len(shares)),
        out_shape=(
            shaped((subj_dev, long, plane, depth)),
            shaped((3, subj_dev, long, plane, depth)),
            shaped((subj_dev, long, plane, depth)),
            shaped((3, subj_dev, rows + 2, plane, depth)),
            sums,
            sums,
        ),
        in_specs=[SMEM] * 3 + [VMEM] * len(arrays) + [ANY] * 2,
        out_specs=(VMEM,) * 6,
        scratch_shapes=[
            pltpu.VMEM((spaces * total, plane, depth), weights.dtype),
            pltpu.VMEM((3, subj_dev, long, plane, depth), jnp.float32),
            pltpu.VMEM(weights.shape, weights.dtype),
            pltpu.VMEM((2,) + side.shape, side.dtype),
            pltpu.SemaphoreType.DMA((8,)),
        ],
        compiler_params=params(),
        name="first",
    )(counts, slots, edge_slots, *arrays, in_hbm(weights), in_hbm(velocity))


def last_kernel(
    mine_ref,
    other_ref,
    warped_ref,
    slopes_ref,
    scale_ref,
    field_ref,
    out_ref,
    keep_ref,
    send_ref,
    update,
    out,
    sems,
):
    _, subj_dev, rows, plane, depth = out.shape
    core = lax.bitwise_and(lax.axis_index("subj"), 1)
    masks = inside((plane, depth), 1.0)
    chunks = sems.shape[0]
    chunk = rows // chunks

    def renew(i, carry):
        mine, other = mine_ref[i].astype(jnp.float32), other_ref[i].astype(jnp.float32)
        current = jnp.concatenate(
            [jnp.where(core == 0, mine, other), jnp.where(core == 0, other, mine)], axis=0
        )
        for s in range(subj_dev):
            g = [slopes_ref[c, s, i + 1] for c in range(3)]
            f = [field_ref[c, s, i] for c in range(3)]
            ratio = (predict(warped_ref[s, i + 1], g, f) - current) * scale_ref[s, i + 1]
            for c in range(3):
                update[c, s, i] = g[c] * ratio
        return carry

    lax.fori_loop(0, rows + 2, renew, 0, unroll=11)

    def move(r, carry):
        total = None
        for s in range(subj_dev):
            g = [slopes_ref[c, s, r + EDGE] for c in range(3)]
            f = []
            for c in range(3):
                delta = smooth(update[c, s, r], update[c, s, r + 1], update[c, s, r + 2], masks)
                f.append(field_ref[c, s, r + 1] - delta)
                out[c, s, r] = f[c]
            p = predict(warped_ref[s, r + EDGE], g, f)
            total = p if total is None else total + p
        quarter = plane // 4
        low, high = total[: 2 * quarter], total[2 * quarter :]
        upper = lax.broadcasted_iota(jnp.int32, low.shape, 0) >= quarter
        even = jnp.where(upper, pltpu.roll(high, quarter, 0), low)
        odd = jnp.where(upper, high, pltpu.roll(low, quarter, 0))
        keep_ref[r] = jnp.where(core == 0, even, odd)
        send_ref[r] = jnp.where(core == 0, odd, even)
        return carry

    copies = []
    for i in range(chunks):
        lax.fori_loop(i * chunk, (i + 1) * chunk, move, 0, unroll=16)
        part = pl.ds(i * chunk, chunk)
        copy = pltpu.make_async_copy(out.at[:, :, part], out_ref.at[:, :, part], sems.at[i])
        copy.start()
        copies.append(copy)
    for copy in copies:
        copy.wait()


def last(mine, other, warped, slopes_all, scale, field, rows):
    _, subj_dev, _, plane, depth = field.shape
    shape = (3, subj_dev, rows, plane, depth)
    sums = shaped((rows, plane // 2, depth))
    return pl.pallas_call(
        last_kernel,
        out_shape=(shaped(shape), sums, sums),
        in_specs=[VMEM] * 6,
        out_specs=(ANY, VMEM, VMEM),
        scratch_shapes=[
            pltpu.VMEM(field.shape, jnp.float32),
            pltpu.VMEM(shape, jnp.float32),
            pltpu.SemaphoreType.DMA((4,)),
        ],
        compiler_params=params(),
        name="last",
    )(mine, other, warped, slopes_all, scale, field)


def fold_kernel(keep_ref, got_ref, own_ref, away_ref):
    second = lax.shift_right_logical(lax.axis_index("subj"), 1) == 1
    quarter = own_ref.shape[1]

    def row(r, carry):
        total = keep_ref[r] + got_ref[r]
        low, high = total[:quarter], total[quarter:]
        own_ref[r] = jnp.where(second, high, low)
        away_ref[r] = jnp.where(second, low, high)
        return carry

    lax.fori_loop(0, keep_ref.shape[0], row, 0, unroll=8)


def fold(keep, got):
    rows, half, depth = keep.shape
    part = shaped((rows, half // 2, depth))
    return pl.pallas_call(
        fold_kernel,
        out_shape=(part, part),
        in_specs=[VMEM] * 2,
        out_specs=(VMEM,) * 2,
        compiler_params=params(),
        name="fold",
    )(keep, got)


def swap(value, axis, mask):
    count = lax.axis_size(axis)
    return lax.ppermute(value, axis, [(i, i ^ mask) for i in range(count)])


def body(images, velocity, weights, template, owners, local_rows, tile_counts):
    spaces = lax.axis_size("space")
    groups = lax.axis_size("subj")
    subj_dev, rows, plane, depth = images.shape
    cap = subj_dev * (2 * rows // spaces)
    subjects = subj_dev * groups
    counts = jnp.swapaxes(tile_counts, 0, 1)

    request, slots, held = plan(
        counts,
        jnp.swapaxes(owners, 1, 2),
        local_rows,
        images.reshape(subj_dev * rows, plane, depth),
        template,
        cap,
        spaces,
    )
    answers = lax.all_to_all(request, "space", split_axis=0, concat_axis=0, tiled=True)

    base = spaces // 2
    total = cap + 2 * EDGE * subj_dev
    short = cap - cap // 8
    sizes = [total] * base + [short] * (spaces - base)
    sends, overs, edge_slots, side, ends = pick(
        answers, held, template, velocity, weights, cap, sizes
    )
    far = [swap(sends[k], "space", k) for k in range(base, spaces)]
    shares = [ends] + [swap(ends, "subj", k) for k in range(1, groups)]
    near = [sends[0]] + [swap(sends[k], "space", k) for k in range(1, base)]
    others = [(i, i + 1) for i in range(1, spaces - 1, 2)]
    side = lax.ppermute(side, "space", others + [(j, i) for i, j in others])
    over = functools.reduce(jnp.maximum, [share[-1, 0, 0] for share in shares])
    overs = list(overs)
    overs, far, near[1:], side = lax.optimization_barrier((overs, far, near[1:], side))
    def again(state):
        parts = [swap(part, "space", base + i) for i, part in enumerate(state[1])]
        return 0.0, parts

    _, overs = lax.while_loop(lambda state: state[0] > 0, again, (over, overs))

    warped, slopes_all, scale, field, keep, send = first(
        counts, slots, edge_slots, near + far, overs, shares, side, weights, velocity
    )
    share = keep + swap(send, "subj", 1)
    mask = 2
    while mask < groups:
        share = share + swap(share.astype(jnp.bfloat16), "subj", mask).astype(jnp.float32)
        mask = 2 * mask
    mine = (share / subjects).astype(jnp.bfloat16)
    other = swap(mine, "subj", 1)

    field, keep, send = last(mine, other, warped, slopes_all, scale, field, rows)
    if groups == 4:
        own, away = fold(keep, swap(send, "subj", 1))
        result = (own + swap(away, "subj", 2)) / subjects
    else:
        quarter = plane // 4
        core = lax.bitwise_and(lax.axis_index("subj"), 1)
        even = jnp.where(core == 0, keep, send)
        odd = jnp.where(core == 0, send, keep)
        full = jnp.concatenate(
            [even[:, :quarter], odd[:, :quarter], even[:, quarter:], odd[:, quarter:]], axis=1
        )
        result = lax.psum_scatter(full, "subj", scatter_dimension=1, tiled=True) / subjects
    return field, result


def solution(mesh):
    in_specs = (
        P("subj", "space", None, None),
        P(None, "subj", "space", None, None),
        P(None, "subj", "space", None, None),
        P("space", "subj", None),
        P("subj", "space", None),
        P("subj", "space"),
        P("subj", "space"),
    )
    out_specs = (P(None, "subj", "space", None, None), P("space", "subj", None))
    return jax.shard_map(body, mesh=mesh, in_specs=in_specs, out_specs=out_specs, check_vma=False)
```

profile of v0, /device:TPU:0, one launch (start us, length us, event | category | flops | bytes accessed | tf_op | source)
XLA Modules:
  0.0 74.5 jit_solution(16870718931396052636)
XLA Ops:
  0.6 1.2 %plan.1 = (f32[8,16,128]{2,1,0:T(8,128)S(1)}, s32[2,64]{1,0:T(2,128)S(1)}, bf16[128,16,128]{2,1,0:T(8,128)(2,1)S(1)}) custom-call(s32[1,2]{1,0:T(1,128)} %bitcast.6, s32[2,1,64]{2,1,0:T(1,128)} %bitcast.9, s32[2,64]{1,0:T(2,128)} %rows_in.1, bf16[128,16,128]{2,1,0:T(8,128)(2,1)} %bitcast.8, f32[64,4,128]{2,1,0:T(4,128)} %template_ref.3), custom_call_target="tpu_custom_call" | custom-call | tf_op jit(solution)/shard_map/plan/pallas_call | solution.py:155
  1.8 14.0 %all_to_all.5.answers_ref = f32[8,16,128]{2,1,0:T(8,128)S(1)} all-to-all(f32[8,16,128]{2,1,0:T(8,128)S(1)} %get-tuple-element.73), channel_id=1, replica_groups=mesh['subj'=4,'space'=8] {'space'}, dimensions={0} | all-to-all | bytes 131072 | tf_op jit(solution)/shard_map/all_to_all | solution.py:690
  15.8 0.0 copy-start
  15.8 2.3 %pick.1 = (bf16[40,16,128]{2,1,0:T(8,128)(2,1)S(1)}, bf16[64,16,128]{2,1,0:T(8,128)(2,1)S(1)}, bf16[40,16,128]{2,1,0:T(8,128)(2,1)S(1)}, bf16[40,16,128]{2,1,0:T...) custom-call(f32[8,16,128]{2,1,0:T(8,128)S(1)} %all_to_all.5.answers_, ...), custom_call_target="tpu_custom_call" | custom-call | tf_op jit(solution)/shard_map/pick/pallas_call | solution.py:296
  18.2 0.6 collective-permute-start.4
  18.7 0.7 collective-permute-start.11
  19.4 0.1 collective-permute-start.14
  19.5 4.8 %collective-permute-start.5 = (bf16[28,16,128]{2,1,0:T(8,128)(2,1)S(1)}, bf16[28,16,128]{2,1,0:T(8,128)(2,1)S(1)}, u32[]{:S(2)}, u32[]{:S(2)}) collective-permute-start(bf16[28,16,128]{2,1,0:T(8,128)(2,1)S(1)} %get-tuple-element.82), channel_id=1, source_target_pairs={{0,5},{1,4},{2,7},{3,6},{4,1},{5,0},{6,3},{7,2},{8,13},{9,12},{10,... | collective-permute-start | bytes 344072 | tf_op jit(solution)/shard_map/ppermute | solution.py:670
  24.3 0.4 collective-permute-start.8
  24.7 0.0 collective-permute-done.11.refs_19_
  24.7 1.5 %collective-permute-start.13 = (f32[69,4,128]{2,1,0:T(4,128)S(1)}, f32[69,4,128]{2,1,0:T(4,128)S(1)}, u32[]{:S(2)}, u32[]{:S(2)}) collective-permute-start(f32[69,4,128]{2,1,0:T(4,128)S(1)} %get-tuple-element.96.refs_15_), channel_id=1, source_target_pairs={{0,16},{8,24},{16,0},{24,8},{1,17},{9,25},{17,1},{25,9},{2,18},{10... | collective-permute-start | bytes 423944 | tf_op jit(solution)/shard_map/ppermute | solution.py:670
  26.1 0.0 collective-permute-done.4.refs_7_
  26.1 0.0 collective-permute-start.12
  26.1 1.4 %collective-permute-done.5.refs_8_ = bf16[28,16,128]{2,1,0:T(8,128)(2,1)S(1)} collective-permute-done((bf16[28,16,128]{2,1,0:T(8,128)(2,1)S(1)}, bf16[28,16,128]{2,1,0:T(8,128)(2,1)S(1)}, u32[]{:S(2)}, u32[]{:S(2)}) %collective-permute-start.5) | collective-permute-done | bytes 114720 | tf_op jit(solution)/shard_map/ppermute | solution.py:670
  27.5 2.6 %collective-permute-start.9 = (bf16[40,16,128]{2,1,0:T(8,128)(2,1)S(1)}, bf16[40,16,128]{2,1,0:T(8,128)(2,1)S(1)}, u32[]{:S(2)}, u32[]{:S(2)}) collective-permute-start(bf16[40,16,128]{2,1,0:T(8,128)(2,1)S(1)} %get-tuple-element.86), channel_id=1, source_target_pairs={{0,2},{1,3},{2,0},{3,1},{4,6},{5,7},{6,4},{7,5},{8,10},{9,11},{10,... | collective-permute-start | bytes 491528 | tf_op jit(solution)/shard_map/ppermute | solution.py:670
  30.2 0.0 collective-permute-done.14.refs_18_
  30.2 4.1 %collective-permute-start.10 = (bf16[40,16,128]{2,1,0:T(8,128)(2,1)S(1)}, bf16[40,16,128]{2,1,0:T(8,128)(2,1)S(1)}, u32[]{:S(2)}, u32[]{:S(2)}) collective-permute-start(bf16[40,16,128]{2,1,0:T(8,128)(2,1)S(1)} %get-tuple-element.87), channel_id=1, source_target_pairs={{0,3},{1,2},{2,1},{3,0},{4,7},{5,6},{6,5},{7,4},{8,11},{9,10},{10,... | collective-permute-start | bytes 491528 | tf_op jit(solution)/shard_map/ppermute | solution.py:670
  34.2 0.0 collective-permute-done.13.refs_17_
  34.2 0.3 collective-permute-start.6
  34.5 0.0 collective-permute-done.12.refs_16_
  34.5 2.9 %collective-permute-start.7 = (bf16[28,16,128]{2,1,0:T(8,128)(2,1)S(1)}, bf16[28,16,128]{2,1,0:T(8,128)(2,1)S(1)}, u32[]{:S(2)}, u32[]{:S(2)}) collective-permute-start(bf16[28,16,128]{2,1,0:T(8,128)(2,1)S(1)} %get-tuple-element.84), channel_id=1, source_target_pairs={{0,7},{1,6},{2,5},{3,4},{4,3},{5,2},{6,1},{7,0},{8,15},{9,14},{10,... | collective-permute-start | bytes 344072 | tf_op jit(solution)/shard_map/ppermute | solution.py:670
  37.4 0.5 slice.12
  37.9 0.5 slice.16
  39.8 0.5 slice.17
  40.9 0.5 slice.18
  42.1 3.9 %collective-permute-done.6.refs_9_ = bf16[28,16,128]{2,1,0:T(8,128)(2,1)S(1)} collective-permute-done((bf16[28,16,128]{2,1,0:T(8,128)(2,1)S(1)}, bf16[28,16,128]{2,1,0:T(8,128)(2,1)S(1)}, u32[]{:S(2)}, u32[]{:S(2)}) %collective-permute-start.6) | collective-permute-done | bytes 114720 | tf_op jit(solution)/shard_map/ppermute | solution.py:670
  46.0 0.2 collective-permute-done.7.refs_10_
  46.2 0.0 collective-permute-done.9.refs_5_
  46.2 0.9 %collective-permute-done.10.refs_6_ = bf16[40,16,128]{2,1,0:T(8,128)(2,1)S(1)} collective-permute-done((bf16[40,16,128]{2,1,0:T(8,128)(2,1)S(1)}, bf16[40,16,128]{2,1,0:T(8,128)(2,1)S(1)}, u32[]{:S(2)}, u32[]{:S(2)}) %collective-permute-start.10) | collective-permute-done | bytes 163872 | tf_op jit(solution)/shard_map/ppermute | solution.py:670
  47.1 0.0 collective-permute-done.8.refs_4_
  47.1 0.0 copy-done
  47.1 7.3 %first.1 = (f32[2,68,16,128]{3,2,1,0:T(8,128)S(1)}, f32[3,2,68,16,128]{4,3,2,1,0:T(8,128)S(1)}, f32[2,68,16,128]{3,2,1,0:T(8,128)S(1)}, f32[3,2,66,16,128]{4,3,2...) custom-call(s32[1,2]{1,0:T(1,128)S(1)} %bitcast.7, s32[2,64]{1,0:T(2,128)S(1)} %get-tuple-element.72.refs_1_, ...), custom_call_target="tpu_custom_call" | custom-call | tf_op jit(solution)/shard_map/first/pallas_call | solution.py:532
  54.5 0.1 collective-permute-start.15
  54.5 1.5 %collective-permute-done.15 = f32[66,8,128]{2,1,0:T(8,128)S(1)} collective-permute-done((f32[66,8,128]{2,1,0:T(8,128)S(1)}, f32[66,8,128]{2,1,0:T(8,128)S(1)}, u32[]{:S(2)}, u32[]{:S(2)}) %collective-permute-start.15) | collective-permute-done | bytes 270368 | tf_op jit(solution)/shard_map/ppermute | solution.py:670
  56.1 1.3 %collective-permute-start.16 = (bf16[66,8,128]{2,1,0:T(8,128)(2,1)S(1)}, bf16[66,8,128]{2,1,0:T(8,128)(2,1)S(1)}, u32[]{:S(2)}, u32[]{:S(2)}) collective-permute-start(bf16[66,8,128]{2,1,0:T(8,128)(2,1)S(1)} %get-tuple-element.127), channel_id=1, source_target_pairs={{0,16},{8,24},{16,0},{24,8},{1,17},{9,25},{17,1},{25,9},{2,18},{10... | collective-permute-start | bytes 405512 | tf_op jit(solution)/shard_map/ppermute | solution.py:670
  57.4 4.4 %collective-permute-done.16 = bf16[66,8,128]{2,1,0:T(8,128)(2,1)S(1)} collective-permute-done((bf16[66,8,128]{2,1,0:T(8,128)(2,1)S(1)}, bf16[66,8,128]{2,1,0:T(8,128)(2,1)S(1)}, u32[]{:S(2)}, u32[]{:S(2)}) %collective-permute-start.16) | collective-permute-done | bytes 135200 | tf_op jit(solution)/shard_map/ppermute | solution.py:670
  61.9 0.1 collective-permute-start.17
  61.9 1.3 %collective-permute-done.17.other_ref = bf16[66,8,128]{2,1,0:T(8,128)(2,1)S(1)} collective-permute-done((bf16[66,8,128]{2,1,0:T(8,128)(2,1)S(1)}, bf16[66,8,128]{2,1,0:T(8,128)(2,1)S(1)}, u32[]{:S(2)}, u32[]{:S(2)}) %collective-permute-start.17) | collective-permute-done | bytes 135200 | tf_op jit(solution)/shard_map/ppermute | solution.py:670
  63.3 3.2 %last.1 = (f32[3,2,64,16,128]{4,3,2,1,0:T(8,128)}, f32[64,8,128]{2,1,0:T(8,128)S(1)}, f32[64,8,128]{2,1,0:T(8,128)S(1)}) custom-call(bf16[66,8,128]{2,1,0:T(8,128)(2,1)S(1)} %multiply_convert_fusion.mine_ref, bf16[66,8,128]{2,1,0:T(8,128)(2,1)S(1)} %collective-permute-done.17.other_ref, f32[2,68,16,128]{3,2,1,0:T(8,128)S(1)} %get-tuple-element.108.warped_ref, ...), custom_call_target="tpu_custom_call" | custom-call | tf_op jit(solution)/shard_map/last/pallas_call | solution.py:626
  66.5 0.2 collective-permute-start.18
  66.7 1.4 %collective-permute-done.18.got_ref = f32[64,8,128]{2,1,0:T(8,128)S(1)} collective-permute-done((f32[64,8,128]{2,1,0:T(8,128)S(1)}, f32[64,8,128]{2,1,0:T(8,128)S(1)}, u32[]{:S(2)}, u32[]{:S(2)}) %collective-permute-start.18) | collective-permute-done | bytes 262176 | tf_op jit(solution)/shard_map/ppermute | solution.py:670
  68.1 0.1 fold.1
  68.2 1.3 %collective-permute-start.19 = (f32[64,4,128]{2,1,0:T(4,128)S(1)}, f32[64,4,128]{2,1,0:T(4,128)S(1)}, u32[]{:S(2)}, u32[]{:S(2)}) collective-permute-start(f32[64,4,128]{2,1,0:T(4,128)S(1)} %get-tuple-element.116), channel_id=1, source_target_pairs={{0,16},{8,24},{16,0},{24,8},{1,17},{9,25},{17,1},{25,9},{2,18},{10... | collective-permute-start | bytes 393224 | tf_op jit(solution)/shard_map/ppermute | solution.py:670
  69.5 4.3 %collective-permute-done.19 = f32[64,4,128]{2,1,0:T(4,128)S(1)} collective-permute-done((f32[64,4,128]{2,1,0:T(4,128)S(1)}, f32[64,4,128]{2,1,0:T(4,128)S(1)}, u32[]{:S(2)}, u32[]{:S(2)}) %collective-permute-start.19) | collective-permute-done | bytes 131104 | tf_op jit(solution)/shard_map/ppermute | solution.py:670
  73.8 0.7 add_multiply_fusion
  (3 shorter events, 0.1 us)
Async XLA Ops:
  15.8 31.3 %copy-start = (s32[2,1]{0,1:T(1,128)S(1)}, s32[2,1]{0,1:T(1,128)}, u32[]{:S(2)}) copy-start(s32[2,1]{0,1:T(1,128)} %param.15) | copy-start | bytes 28
  18.2 8.0 %collective-permute-start.4 = (bf16[28,16,128]{2,1,0:T(8,128)(2,1)S(1)}, bf16[28,16,128]{2,1,0:T(8,128)(2,1)S(1)}, u32[]{:S(2)}, u32[]{:S(2)}) collective-permute-start(bf16[28,16,128]{2,1,0:T(8,128)(2,1)S(1)} %get-tuple-element.81), channel_id=1, source_target_pairs={{0,4},{1,5},{2,6},{3,7},{4,0},{5,1},{6,2},{7,3},{8,12},{9,13},{10,... | collective-permute-start | bytes 344072 | tf_op jit(solution)/shard_map/ppermute | solution.py:670
  18.7 5.9 %collective-permute-start.11 = (bf16[24,16,128]{2,1,0:T(8,128)(2,1)S(1)}, bf16[24,16,128]{2,1,0:T(8,128)(2,1)S(1)}, u32[]{:S(2)}, u32[]{:S(2)}) collective-permute-start(bf16[24,16,128]{2,1,0:T(8,128)(2,1)S(1)} %get-tuple-element.88), channel_id=1, source_target_pairs={{1,2},{3,4},{5,6},{2,1},{4,3},{6,5},{9,10},{11,12},{13,14},{10,9},... | collective-permute-start | bytes 294920 | tf_op jit(solution)/shard_map/ppermute | solution.py:703
  19.4 10.8 %collective-permute-start.14 = (f32[69,4,128]{2,1,0:T(4,128)S(1)}, f32[69,4,128]{2,1,0:T(4,128)S(1)}, u32[]{:S(2)}, u32[]{:S(2)}) collective-permute-start(f32[69,4,128]{2,1,0:T(4,128)S(1)} %get-tuple-element.96.refs_15_), channel_id=1, source_target_pairs={{0,24},{8,16},{16,8},{24,0},{1,25},{9,17},{17,9},{25,1},{2,26},{10... | collective-permute-start | bytes 423944 | tf_op jit(solution)/shard_map/ppermute | solution.py:670
  19.5 8.1 %collective-permute-start.5 = (bf16[28,16,128]{2,1,0:T(8,128)(2,1)S(1)}, bf16[28,16,128]{2,1,0:T(8,128)(2,1)S(1)}, u32[]{:S(2)}, u32[]{:S(2)}) collective-permute-start(bf16[28,16,128]{2,1,0:T(8,128)(2,1)S(1)} %get-tuple-element.82), channel_id=1, source_target_pairs={{0,5},{1,4},{2,7},{3,6},{4,1},{5,0},{6,3},{7,2},{8,13},{9,12},{10,... | collective-permute-start | bytes 344072 | tf_op jit(solution)/shard_map/ppermute | solution.py:670
  24.3 22.8 %collective-permute-start.8 = (bf16[64,16,128]{2,1,0:T(8,128)(2,1)S(1)}, bf16[64,16,128]{2,1,0:T(8,128)(2,1)S(1)}, u32[]{:S(2)}, u32[]{:S(2)}) collective-permute-start(bf16[64,16,128]{2,1,0:T(8,128)(2,1)S(1)} %get-tuple-element.85), channel_id=1, source_target_pairs={{0,1},{1,0},{2,3},{3,2},{4,5},{5,4},{6,7},{7,6},{8,9},{9,8},{10,11... | collective-permute-start | bytes 786440 | tf_op jit(solution)/shard_map/ppermute | solution.py:670
  24.7 9.6 %collective-permute-start.13 = (f32[69,4,128]{2,1,0:T(4,128)S(1)}, f32[69,4,128]{2,1,0:T(4,128)S(1)}, u32[]{:S(2)}, u32[]{:S(2)}) collective-permute-start(f32[69,4,128]{2,1,0:T(4,128)S(1)} %get-tuple-element.96.refs_15_), channel_id=1, source_target_pairs={{0,16},{8,24},{16,0},{24,8},{1,17},{9,25},{17,1},{25,9},{2,18},{10... | collective-permute-start | bytes 423944 | tf_op jit(solution)/shard_map/ppermute | solution.py:670
  26.1 8.4 %collective-permute-start.12 = (f32[69,4,128]{2,1,0:T(4,128)S(1)}, f32[69,4,128]{2,1,0:T(4,128)S(1)}, u32[]{:S(2)}, u32[]{:S(2)}) collective-permute-start(f32[69,4,128]{2,1,0:T(4,128)S(1)} %get-tuple-element.96.refs_15_), channel_id=1, source_target_pairs={{0,8},{8,0},{16,24},{24,16},{1,9},{9,1},{17,25},{25,17},{2,10},{10... | collective-permute-start | bytes 423944 | tf_op jit(solution)/shard_map/ppermute | solution.py:670
  27.5 18.7 %collective-permute-start.9 = (bf16[40,16,128]{2,1,0:T(8,128)(2,1)S(1)}, bf16[40,16,128]{2,1,0:T(8,128)(2,1)S(1)}, u32[]{:S(2)}, u32[]{:S(2)}) collective-permute-start(bf16[40,16,128]{2,1,0:T(8,128)(2,1)S(1)} %get-tuple-element.86), channel_id=1, source_target_pairs={{0,2},{1,3},{2,0},{3,1},{4,6},{5,7},{6,4},{7,5},{8,10},{9,11},{10,... | collective-permute-start | bytes 491528 | tf_op jit(solution)/shard_map/ppermute | solution.py:670
  30.2 16.9 %collective-permute-start.10 = (bf16[40,16,128]{2,1,0:T(8,128)(2,1)S(1)}, bf16[40,16,128]{2,1,0:T(8,128)(2,1)S(1)}, u32[]{:S(2)}, u32[]{:S(2)}) collective-permute-start(bf16[40,16,128]{2,1,0:T(8,128)(2,1)S(1)} %get-tuple-element.87), channel_id=1, source_target_pairs={{0,3},{1,2},{2,1},{3,0},{4,7},{5,6},{6,5},{7,4},{8,11},{9,10},{10,... | collective-permute-start | bytes 491528 | tf_op jit(solution)/shard_map/ppermute | solution.py:670
  34.2 11.8 %collective-permute-start.6 = (bf16[28,16,128]{2,1,0:T(8,128)(2,1)S(1)}, bf16[28,16,128]{2,1,0:T(8,128)(2,1)S(1)}, u32[]{:S(2)}, u32[]{:S(2)}) collective-permute-start(bf16[28,16,128]{2,1,0:T(8,128)(2,1)S(1)} %get-tuple-element.83), channel_id=1, source_target_pairs={{0,6},{1,7},{2,4},{3,5},{4,2},{5,3},{6,0},{7,1},{8,14},{9,15},{10,... | collective-permute-start | bytes 344072 | tf_op jit(solution)/shard_map/ppermute | solution.py:670
  34.5 11.7 %collective-permute-start.7 = (bf16[28,16,128]{2,1,0:T(8,128)(2,1)S(1)}, bf16[28,16,128]{2,1,0:T(8,128)(2,1)S(1)}, u32[]{:S(2)}, u32[]{:S(2)}) collective-permute-start(bf16[28,16,128]{2,1,0:T(8,128)(2,1)S(1)} %get-tuple-element.84), channel_id=1, source_target_pairs={{0,7},{1,6},{2,5},{3,4},{4,3},{5,2},{6,1},{7,0},{8,15},{9,14},{10,... | collective-permute-start | bytes 344072 | tf_op jit(solution)/shard_map/ppermute | solution.py:670
  54.5 1.6 %collective-permute-start.15 = (f32[66,8,128]{2,1,0:T(8,128)S(1)}, f32[66,8,128]{2,1,0:T(8,128)S(1)}, u32[]{:S(2)}, u32[]{:S(2)}) collective-permute-start(f32[66,8,128]{2,1,0:T(8,128)S(1)} %get-tuple-element.107), channel_id=1, source_target_pairs={{0,8},{8,0},{16,24},{24,16},{1,9},{9,1},{17,25},{25,17},{2,10},{10... | collective-permute-start | bytes 811016 | tf_op jit(solution)/shard_map/ppermute | solution.py:670
  56.1 5.7 %collective-permute-start.16 = (bf16[66,8,128]{2,1,0:T(8,128)(2,1)S(1)}, bf16[66,8,128]{2,1,0:T(8,128)(2,1)S(1)}, u32[]{:S(2)}, u32[]{:S(2)}) collective-permute-start(bf16[66,8,128]{2,1,0:T(8,128)(2,1)S(1)} %get-tuple-element.127), channel_id=1, source_target_pairs={{0,16},{8,24},{16,0},{24,8},{1,17},{9,25},{17,1},{25,9},{2,18},{10... | collective-permute-start | bytes 405512 | tf_op jit(solution)/shard_map/ppermute | solution.py:670
  61.9 1.4 %collective-permute-start.17 = (bf16[66,8,128]{2,1,0:T(8,128)(2,1)S(1)}, bf16[66,8,128]{2,1,0:T(8,128)(2,1)S(1)}, u32[]{:S(2)}, u32[]{:S(2)}) collective-permute-start(bf16[66,8,128]{2,1,0:T(8,128)(2,1)S(1)} %multiply_convert_fusion.mine_ref), channel_id=1, source_target_pairs={{0,8},{8,0},{16,24},{24,16},{1,9},{9,1},{17,25},{25,17},{2,10},{10... | collective-permute-start | bytes 405512 | tf_op jit(solution)/shard_map/ppermute | solution.py:670
  66.5 1.6 %collective-permute-start.18 = (f32[64,8,128]{2,1,0:T(8,128)S(1)}, f32[64,8,128]{2,1,0:T(8,128)S(1)}, u32[]{:S(2)}, u32[]{:S(2)}) collective-permute-start(f32[64,8,128]{2,1,0:T(8,128)S(1)} %get-tuple-element.114), channel_id=1, source_target_pairs={{0,8},{8,0},{16,24},{24,16},{1,9},{9,1},{17,25},{25,17},{2,10},{10... | collective-permute-start | bytes 786440 | tf_op jit(solution)/shard_map/ppermute | solution.py:670
  68.2 5.6 %collective-permute-start.19 = (f32[64,4,128]{2,1,0:T(4,128)S(1)}, f32[64,4,128]{2,1,0:T(4,128)S(1)}, u32[]{:S(2)}, u32[]{:S(2)}) collective-permute-start(f32[64,4,128]{2,1,0:T(4,128)S(1)} %get-tuple-element.116), channel_id=1, source_target_pairs={{0,16},{8,24},{16,0},{24,8},{1,17},{9,25},{17,1},{25,9},{2,18},{10... | collective-permute-start | bytes 393224 | tf_op jit(solution)/shard_map/ppermute | solution.py:670
where the time goes:
time: 74.7 us; the launch traced here: 74.5 us
  starting transfers between devices  20.9 us (28%)
  waiting for transfers between devices  19.3 us (26%)
  Pallas kernels  14.1 us (19%)
  blocking collectives  14 us (19%)
  between operations  3.33 us (4%)
  local copies, waits for them, and re-layouts  2.05 us (3%)
  other arithmetic  0.79 us (1%)
    ppermute x15, starting transfers between devices, swap(): return lax.ppermute(value, axis, [(i, i ^ mask) for i in range(count)])  20.2 us
    ppermute x15, waiting for transfers between devices, swap(): return lax.ppermute(value, axis, [(i, i ^ mask) for i in range(count)])  19.3 us
    all_to_all x1, blocking collectives, body(): lax.all_to_all(request, 'space', split_axis=0, concat_axis=0, tiled=True)  14 us
    pallas_call x1, Pallas kernels, first(): pl.pallas_call(functools.partial(first_kernel, spaces, spaces - len(overs...  7.34 us
    pallas_call x1, Pallas kernels, last(): pl.pallas_call(last_kernel, out_shape=(shaped(shape), sums, sums), in_spe...  3.21 us
    pallas_call x1, Pallas kernels, pick(): pl.pallas_call(functools.partial(pick_kernel, cap, base, total), out_shap...  2.35 us
    slice x4, local copies, waits for them, and re-layouts, body(): over = functools.reduce(jnp.maximum, [share[-1, 0, 0] for share in shares])  2.05 us
  transfers between devices with their start and end apart: 16, of which 9 were waited for; matrix products, arithmetic and copies ran while one was open for 3% of the time, Pallas kernels for 0%

commit v1 on v0

--- a/solution.py
+++ b/solution.py
@@ -14,7 +14,6 @@
 LIMIT = 24 * 1024 * 1024
 EDGE = 2
 CODES = 48
-HEAD = 8
 COUNTS = 64
 SHIFT = 8
 
@@ -46,20 +45,23 @@
     owners_in,
     rows_in,
     images_ref,
-    template_ref,
+    velocity_ref,
+    weights_ref,
     request_ref,
     slots_ref,
     held_ref,
+    near_ref,
+    side_ref,
     counts_ref,
     owners_ref,
     rows_ref,
-    ends_ref,
+    v_ref,
+    w_ref,
     sems,
 ):
     subj_dev, rows = rows_ref.shape
     spaces = request_ref.shape[0]
-    share = template_ref.shape[1]
-    me = lax.axis_index("space")
+    odd = lax.bitwise_and(lax.axis_index("space"), 1)
     copies = [
         pltpu.make_async_copy(source, target, sems.at[i])
         for i, (source, target) in enumerate(
@@ -67,9 +69,11 @@
                 (counts_in, counts_ref),
                 (owners_in, owners_ref),
                 (rows_in, rows_ref),
-                (template_ref.at[pl.ds(0, EDGE)], ends_ref.at[0]),
-                (template_ref.at[pl.ds(rows - EDGE, EDGE)], ends_ref.at[1]),
                 (images_ref, held_ref),
+                (velocity_ref.at[:, :, pl.ds(0, EDGE)], v_ref.at[1 - odd]),
+                (weights_ref.at[:, :, pl.ds(0, EDGE)], w_ref.at[1 - odd]),
+                (velocity_ref.at[:, :, pl.ds(rows - EDGE, EDGE)], v_ref.at[odd]),
+                (weights_ref.at[:, :, pl.ds(rows - EDGE, EDGE)], w_ref.at[odd]),
             )
         )
     ]
@@ -135,42 +139,45 @@
             )
             code = jnp.sum(code, axis=0, keepdims=True)
             extra = extra + jnp.where((line >= place) & (line < place + EDGE), code, 0)
-    request = (request + jnp.broadcast_to(extra, request.shape)).astype(jnp.float32)
+    request_ref[...] = request + jnp.broadcast_to(extra, request.shape)
     for copy in copies[3:]:
         copy.wait()
-    for o in range(spaces):
-        request_ref[o, :HEAD] = jnp.broadcast_to(request[o : o + 1], (HEAD, LANES))
-        for r in range(EDGE):
-            at = HEAD + r * share
-            request_ref[o, at : at + share] = jnp.where(o < me, ends_ref[0, r], ends_ref[1, r])
-        if HEAD + EDGE * share < request_ref.shape[1]:
-            rest = request_ref.shape[1] - HEAD - EDGE * share
-            request_ref[o, HEAD + EDGE * share :] = jnp.zeros((rest, LANES), jnp.float32)
-
-
-def plan(counts, owners, local_rows, images, template, cap, spaces):
+    for place, out in enumerate((near_ref, side_ref)):
+        i = 0
+        for c in range(3):
+            for s in range(subj_dev):
+                for r in range(EDGE):
+                    out[i] = v_ref[place, c, s, r].astype(out.dtype)
+                    out[i + 1] = w_ref[place, c, s, r]
+                    i = i + 2
+
+
+def plan(counts, owners, local_rows, images, velocity, weights, cap, spaces):
     subj_dev, rows = local_rows.shape
-    share = template.shape[1]
-    lines = HEAD + -(-EDGE * share // 8) * 8
+    tile = velocity.shape[3:]
+    edge = shaped((2 * EDGE * 3 * subj_dev,) + tile, weights.dtype)
     return pl.pallas_call(
         functools.partial(plan_kernel, cap),
         out_shape=(
-            shaped((spaces, lines, LANES)),
+            shaped((spaces, LANES), jnp.int32),
             shaped((subj_dev, rows), jnp.int32),
             pltpu.VMEM(images.shape, images.dtype),
+            edge,
+            edge,
         ),
-        in_specs=[ANY] * 5,
-        out_specs=(VMEM, VMEM, VMEM),
+        in_specs=[ANY] * 6,
+        out_specs=(VMEM,) * 5,
         scratch_shapes=[
             pltpu.SMEM(counts.shape, jnp.int32),
             pltpu.VMEM(owners.shape, jnp.int32),
             pltpu.VMEM(local_rows.shape, jnp.int32),
-            pltpu.VMEM((2, EDGE, share, LANES), jnp.float32),
-            pltpu.SemaphoreType.DMA((6,)),
+            pltpu.VMEM((2, 3, subj_dev, EDGE) + tile, velocity.dtype),
+            pltpu.VMEM((2, 3, subj_dev, EDGE) + tile, weights.dtype),
+            pltpu.SemaphoreType.DMA((8,)),
         ],
         compiler_params=params(),
         name="plan",
-    )(*map(in_hbm, (counts, owners, local_rows, images, template)))
+    )(*map(in_hbm, (counts, owners, local_rows, images, velocity, weights)))
 
 
 def edge_codes(wanted_ref, me, subj_dev):
@@ -202,38 +209,33 @@
     return jnp.max(jnp.max(over, axis=0, keepdims=True), axis=1, keepdims=True)
 
 
-def pick_kernel(cap, base, total, answers_ref, images_ref, template_ref, velocity_ref, weights_ref, *refs):
-    spaces = answers_ref.shape[0]
+def whole_row(shares, r, position):
+    parts = [share[r] for share in shares]
+    mask = 1
+    while mask < len(shares):
+        turned = lax.bitwise_and(position, mask) > 0
+        parts = [jnp.where(turned, parts[i ^ mask], part) for i, part in enumerate(parts)]
+        mask = 2 * mask
+    return jnp.concatenate(parts, axis=0)
+
+
+def carries(spaces):
+    return [k for k in range(3, spaces) if k & (k + 1) == 0]
+
+
+def pick_kernel(cap, base, total, groups, wanted_ref, requests_ref, images_ref, near_ref, *refs):
+    shares, refs = refs[:groups], refs[groups + 1 :]
+    spaces = requests_ref.shape[0]
     sends, overs = refs[:spaces], refs[spaces : 2 * spaces - base]
-    edge_slots, side_ref, ends_ref, requests_ref, wanted_ref, used, v_ref, w_ref, sems = refs[-9:]
-    rows, share = template_ref.shape[:2]
-    subj_dev = velocity_ref.shape[1]
-    me = lax.axis_index("space")
+    edge_slots, over_ref, used = refs[-3:]
+    rows = shares[0].shape[0]
+    subj_dev = (total - cap) // (2 * EDGE)
+    me, position = lax.axis_index("space"), lax.axis_index("subj")
     odd = lax.bitwise_and(me, 1)
-    fetches = [pltpu.make_async_copy(template_ref, ends_ref.at[pl.ds(0, rows)], sems.at[0])]
-    for side, begin in enumerate((0, rows - EDGE)):
-        part = pl.ds(begin, EDGE)
-        place = lax.bitwise_xor(odd, 1 - side)
-        for i, (source, target) in enumerate(((velocity_ref, v_ref), (weights_ref, w_ref))):
-            fetches.append(
-                pltpu.make_async_copy(
-                    source.at[:, :, part], target.at[place], sems.at[2 + 2 * side + i]
-                )
-            )
-    for copy in fetches:
-        copy.start()
-    for d in range(spaces):
-        requests_ref[d : d + 1] = answers_ref[d, :1].astype(jnp.int32)
-    move = pltpu.make_async_copy(requests_ref, wanted_ref, sems.at[1])
-    move.start()
-    for side, neighbour in enumerate((jnp.maximum(me - 1, 0), jnp.minimum(me + 1, spaces - 1))):
-        for r in range(EDGE):
-            at = HEAD + r * share
-            ends_ref[rows + side * EDGE + r] = answers_ref[neighbour, at : at + share]
-    move.wait()
+    short = sends[-1].shape[0] - 2 * EDGE
     for k in range(spaces):
         target = lax.bitwise_xor(me, k)
-        size = sends[k].shape[0] if k >= base else total
+        size = short if k >= base else total
 
         def put(c, brick, k=k, size=size):
             if isinstance(c, int):
@@ -262,9 +264,7 @@
                 put(place, images_ref[lax.bitwise_and(code, (1 << SHIFT) - 1)])
 
             place = place + jnp.where(mine, 1, 0)
-    ends_ref[rows + 2 * EDGE] = jnp.broadcast_to(
-        crowded(requests_ref[...], base, sends[-1].shape[0], subj_dev), ends_ref.shape[1:]
-    )
+    over_ref[0] = jnp.max(crowded(requests_ref[...], base, short, subj_dev)).astype(jnp.int32)
     for o in range(spaces):
         used[o] = wanted_ref[me, COUNTS + o]
     for i, (code, valid) in enumerate(edge_codes(wanted_ref, me, subj_dev)):
@@ -272,49 +272,39 @@
         place = used[owner]
         edge_slots[i] = jnp.where(valid, lax.bitwise_xor(owner, me) * total + place, 0)
         used[owner] = place + jnp.where(valid, 1, 0)
-    for copy in fetches:
-        copy.wait()
-    for side, (out, i) in enumerate(((sends[1], total), (side_ref, 0))):
-        for c in range(3):
-            for s in range(subj_dev):
-                for r in range(EDGE):
-                    out[i] = v_ref[side, c, s, r].astype(out.dtype)
-                    out[i + 1] = w_ref[side, c, s, r]
-                    i = i + 2
-
-
-def pick(answers, images, template, velocity, weights, cap, sizes):
-    spaces = answers.shape[0]
-    subj_dev = velocity.shape[1]
-    total = cap + 2 * EDGE * subj_dev
+    for i in range(near_ref.shape[0]):
+        sends[1][total + 2 * EDGE + i] = near_ref[i]
+    for r in range(EDGE):
+        low = whole_row(shares, r, position)
+        high = whole_row(shares, rows - EDGE + r, position)
+        for k in [1, *carries(spaces)]:
+            value = jnp.where((odd == 1) == (k == 1), low, high)
+            at = (short if k >= base else total) + 2 * r
+            rounded = value.astype(sends[k].dtype)
+            sends[k][at] = rounded
+            sends[k][at + 1] = (value - rounded.astype(jnp.float32)).astype(sends[k].dtype)
+
+
+def pick(wanted, images, near, shares, side, cap, sizes):
+    spaces = wanted.shape[0]
+    base = sizes.index(min(sizes))
+    total = sizes[0]
     tile = images.shape[1:]
-    packed = 2 * EDGE * 3 * subj_dev
-    base = sizes.index(min(sizes))
-    longer = [n + packed if k == 1 else n for k, n in enumerate(sizes)]
+    longer = [n + 2 * EDGE * (k == 1 or k in carries(spaces)) for k, n in enumerate(sizes)]
+    longer[1] += near.shape[0]
     outs = [shaped((n,) + tile, images.dtype) for n in longer]
     outs += [shaped((total - n,) + tile, images.dtype) for n in sizes[base:]]
+    edges = total - cap
     got = pl.pallas_call(
-        functools.partial(pick_kernel, cap, base, total),
-        out_shape=outs
-        + [
-            shaped((2 * EDGE * subj_dev,), jnp.int32),
-            shaped((packed,) + tile, images.dtype),
-            shaped((template.shape[0] + 2 * EDGE + 1,) + template.shape[1:]),
-        ],
-        in_specs=[VMEM, VMEM, ANY, ANY, ANY],
-        out_specs=[VMEM] * len(outs) + [SMEM, VMEM, VMEM],
-        scratch_shapes=[
-            pltpu.VMEM((spaces, LANES), jnp.int32),
-            pltpu.SMEM((spaces, LANES), jnp.int32),
-            pltpu.SMEM((spaces,), jnp.int32),
-            pltpu.VMEM((2, 3, subj_dev, EDGE) + tile, velocity.dtype),
-            pltpu.VMEM((2, 3, subj_dev, EDGE) + tile, weights.dtype),
-            pltpu.SemaphoreType.DMA((6,)),
-        ],
+        functools.partial(pick_kernel, cap, base, total, len(shares)),
+        out_shape=outs + [shaped((edges,), jnp.int32), shaped((1,), jnp.int32)],
+        in_specs=[SMEM] + [VMEM] * (3 + len(shares)) + [ANY],
+        out_specs=[VMEM] * len(outs) + [SMEM, SMEM],
+        scratch_shapes=[pltpu.SMEM((spaces,), jnp.int32)],
         compiler_params=params(),
         name="pick",
-    )(answers, images, *map(in_hbm, (template, velocity, weights)))
-    return got[:spaces], got[spaces:-3], *got[-3:]
+    )(wanted, wanted, images, near, *shares, side)
+    return got[:spaces], got[spaces:-2], *got[-2:]
 
 
 def up_x(v):
@@ -398,7 +388,7 @@
     table, update, weights_ref, packs, chunk_sems = refs[9:]
     _, subj_dev, rows, plane, depth = weights_ref.shape
     total = parts[0].shape[0]
-    short = parts[-1].shape[0]
+    short = parts[-1].shape[0] - 2 * EDGE
     cap = total - 2 * EDGE * subj_dev
     me, position = lax.axis_index("space"), lax.axis_index("subj")
     core = lax.bitwise_and(position, 1)
@@ -425,9 +415,20 @@
                 table[k * total + c] = parts[k][c]
             else:
                 table[k * total + c] = overs[k - base][c - short]
-    for i in range(packs.shape[1]):
+    for i in range(side_ref.shape[0]):
+        packs[1 - odd, 2 * EDGE + i] = parts[1][total + 2 * EDGE + i]
+        packs[odd, 2 * EDGE + i] = side_ref[i]
+    for i in range(2 * EDGE):
         packs[1 - odd, i] = parts[1][total + i]
-        packs[odd, i] = side_ref[i]
+        packs[odd, i] = jnp.zeros_like(side_ref[0])
+    other = lax.bitwise_xor(me, me - 1 + 2 * odd)
+    for k in carries(spaces):
+
+        @pl.when(other == k)
+        def _(k=k):
+            for i in range(2 * EDGE):
+                packs[odd, i] = parts[k][(short if k >= base else total) + i]
+
     before_ref, after_ref = packs.at[0], packs.at[1]
     masks, halves = inside((plane, depth), 1.0), inside((plane, depth), 0.5)
 
@@ -442,17 +443,8 @@
             slopes_ref[c, s, e] = g[c]
             update[c, s, e] = g[c] * ratio
 
-    def template_row(r):
-        parts = [shares[k][r] for k in range(groups)]
-        mask = 1
-        while mask < groups:
-            turned = lax.bitwise_and(position, mask) > 0
-            parts = [jnp.where(turned, parts[i ^ mask], part) for i, part in enumerate(parts)]
-            mask = 2 * mask
-        return jnp.concatenate(parts, axis=0)
-
     def row(r, carry):
-        current = template_row(r)
+        current = whole_row(shares, r, position)
         for s in range(subj_dev):
             count = counts_ref[0, s]
             first = lax.shift_right_logical(count, 1)
@@ -477,9 +469,9 @@
     ):
         live = jnp.where(there, 1.0, 0.0).astype(jnp.float32)
         for r in range(EDGE):
-            current = template_row(rows + side * EDGE + r)
+            current = ref[2 * r].astype(jnp.float32) + ref[2 * r + 1].astype(jnp.float32)
             for s in range(subj_dev):
-                at = [2 * ((c * subj_dev + s) * EDGE + r) for c in range(3)]
+                at = [2 * ((c * subj_dev + s + 1) * EDGE + r) for c in range(3)]
                 tile(
                     s,
                     e0 + r,
@@ -497,7 +489,7 @@
 
     for c in range(3):
         for s in range(subj_dev):
-            at = 2 * (c * subj_dev + s) * EDGE
+            at = 2 * (c * subj_dev + s + 1) * EDGE
             field_ref[c, s, 0] = before_ref[at + 2 * (EDGE - 1)].astype(jnp.float32)
             field_ref[c, s, rows + 1] = after_ref[at].astype(jnp.float32)
 
@@ -545,7 +537,7 @@
             pltpu.VMEM((spaces * total, plane, depth), weights.dtype),
             pltpu.VMEM((3, subj_dev, long, plane, depth), jnp.float32),
             pltpu.VMEM(weights.shape, weights.dtype),
-            pltpu.VMEM((2,) + side.shape, side.dtype),
+            pltpu.VMEM((2, side.shape[0] + 2 * EDGE) + side.shape[1:], side.dtype),
             pltpu.SemaphoreType.DMA((8,)),
         ],
         compiler_params=params(),
@@ -678,37 +670,34 @@
     subjects = subj_dev * groups
     counts = jnp.swapaxes(tile_counts, 0, 1)
 
-    request, slots, held = plan(
+    request, slots, held, near_pack, side = plan(
         counts,
         jnp.swapaxes(owners, 1, 2),
         local_rows,
         images.reshape(subj_dev * rows, plane, depth),
-        template,
+        velocity,
+        weights,
         cap,
         spaces,
     )
-    answers = lax.all_to_all(request, "space", split_axis=0, concat_axis=0, tiled=True)
+    others = [(i, i + 1) for i in range(1, spaces - 1, 2)]
+    side = lax.ppermute(side, "space", others + [(j, i) for i, j in others])
+    shares = [template] + [swap(template, "subj", k) for k in range(1, groups)]
+    wanted = lax.all_to_all(request, "space", split_axis=0, concat_axis=0, tiled=True)
 
     base = spaces // 2
     total = cap + 2 * EDGE * subj_dev
     short = cap - cap // 8
     sizes = [total] * base + [short] * (spaces - base)
-    sends, overs, edge_slots, side, ends = pick(
-        answers, held, template, velocity, weights, cap, sizes
-    )
+    sends, overs, edge_slots, over = pick(wanted, held, near_pack, shares, side, cap, sizes)
     far = [swap(sends[k], "space", k) for k in range(base, spaces)]
-    shares = [ends] + [swap(ends, "subj", k) for k in range(1, groups)]
     near = [sends[0]] + [swap(sends[k], "space", k) for k in range(1, base)]
-    others = [(i, i + 1) for i in range(1, spaces - 1, 2)]
-    side = lax.ppermute(side, "space", others + [(j, i) for i, j in others])
-    over = functools.reduce(jnp.maximum, [share[-1, 0, 0] for share in shares])
-    overs = list(overs)
-    overs, far, near[1:], side = lax.optimization_barrier((overs, far, near[1:], side))
+
     def again(state):
         parts = [swap(part, "space", base + i) for i, part in enumerate(state[1])]
-        return 0.0, parts
-
-    _, overs = lax.while_loop(lambda state: state[0] > 0, again, (over, overs))
+        return jnp.int32(0), parts
+
+    _, overs = lax.while_loop(lambda state: state[0] > 0, again, (over[0], list(overs)))
 
     warped, slopes_all, scale, field, keep, send = first(
         counts, slots, edge_slots, near + far, overs, shares, side, weights, velocity

time: 74.7 us -> 72.5 us (0.971)
  waiting for transfers between devices: 19.3 us -> 24.1 us
  starting transfers between devices: 20.9 us -> 17.8 us
  between operations: 3.33 us -> 0.75 us
  local copies, waits for them, and re-layouts: 2.05 us -> 0.01 us
    ppermute x15, waiting for transfers between devices: 19.3 us -> 24.1 us  [swap(): return lax.ppermute(value, axis, [(i, i ^ mask) for i in range(count)])]
    ppermute x15, starting transfers between devices: 20.2 us -> 17.1 us  [swap(): return lax.ppermute(value, axis, [(i, i ^ mask) for i in range(count)])]
    slice x4 -> x0, local copies, waits for them, and re-layouts: 2.05 us -> none  [body(): over = functools.reduce(jnp.maximum, [share[-1, 0, 0] for share in shares])]
  transfers between devices with their start and end apart: 16 -> 16, of which waited for: 9 -> 9; matrix products, arithmetic and copies ran while one was open for 3% -> 0% of each run, Pallas kernels for 0% -> 2%
where the time goes in v1:
time: 72.5 us; the launch traced here: 72.3 us
  waiting for transfers between devices  24.1 us (33%)
  starting transfers between devices  17.8 us (25%)
  Pallas kernels  14.1 us (19%)
  blocking collectives  14.1 us (19%)
  other arithmetic  0.81 us (1%)
  between operations  0.75 us (1%)
    ppermute x15, waiting for transfers between devices, swap(): return lax.ppermute(value, axis, [(i, i ^ mask) for i in range(count)])  24.1 us
    ppermute x15, starting transfers between devices, swap(): return lax.ppermute(value, axis, [(i, i ^ mask) for i in range(count)])  17.1 us
    all_to_all x1, blocking collectives, body(): lax.all_to_all(request, 'space', split_axis=0, concat_axis=0, tiled=True)  14.1 us
    pallas_call x1, Pallas kernels, first(): pl.pallas_call(functools.partial(first_kernel, spaces, spaces - len(overs...  7.2 us
    pallas_call x1, Pallas kernels, last(): pl.pallas_call(last_kernel, out_shape=(shaped(shape), sums, sums), in_spe...  3.21 us
    pallas_call x1, Pallas kernels, pick(): pl.pallas_call(functools.partial(pick_kernel, cap, base, total, len(share...  2.34 us
  transfers between devices with their start and end apart: 16, of which 9 were waited for; matrix products, arithmetic and copies ran while one was open for 0% of the time, Pallas kernels for 2%

profile of v1, /device:TPU:0, one launch (start us, length us, event | category | flops | bytes accessed | tf_op | source)
XLA Modules:
  0.0 72.3 jit_solution(12451289452575848157)
XLA Ops:
  0.6 0.0 copy-start
  0.6 2.4 %collective-permute-start.6 = (f32[64,4,128]{2,1,0:T(4,128)}, f32[64,4,128]{2,1,0:T(4,128)S(1)}, u32[]{:S(2)}, u32[]{:S(2)}) collective-permute-start(f32[64,4,128]{2,1,0:T(4,128)} %refs_15_.1), channel_id=1, source_target_pairs={{0,24},{8,16},{16,8},{24,0},{1,25},{9,17},{17,9},{25,1},{2,26},{10... | collective-permute-start | bytes 393224 | tf_op jit(solution)/shard_map/ppermute | solution.py:662
  3.1 0.6 collective-permute-start.5
  3.7 0.0 collective-permute-start.4
  3.8 0.0 copy-start.1
  3.8 1.3 %plan.1 = (s32[8,128]{1,0:T(8,128)S(1)}, s32[2,64]{1,0:T(2,128)S(1)}, bf16[128,16,128]{2,1,0:T(8,128)(2,1)S(1)}, bf16[24,16,128]{2,1,0:T(8,128)(2,1)S(1)}, bf16[24,16,128]{2,1,0:T(8,128)(2,1)S(1)}) custom-call(s32[1,2]{1,0:T(1,128)} %bitcast.13, s32[2,1,64]{2,1,0:T(1,128)} %bitcast.16, s32[2,64]{1,0:T(2,128)} %rows_in.1, bf16[128,16,128]{2,1,0:T(8,128)(2,1)} %bitcast.15, ...), custom_call_target="tpu_custom_call" | custom-call | tf_op jit(solution)/shard_map/plan/pallas_call | solution.py:159
  5.1 0.7 collective-permute-start.7
  5.7 14.1 %all_to_all.11 = s32[8,1,128]{2,1,0:T(1,128)S(1)} all-to-all(s32[8,1,128]{2,1,0:T(1,128)S(1)} %bitcast.12), channel_id=1, replica_groups=mesh['subj'=4,'space'=8] {'space'}, dimensions={0} | all-to-all | bytes 8192 | tf_op jit(solution)/shard_map/all_to_all | solution.py:686
  19.8 0.0 collective-permute-done.7.refs_4_.refs_19_
  19.8 0.0 collective-permute-done.6.refs_3_.refs_18_
  19.8 0.0 collective-permute-done.5.refs_2_.refs_17_
  19.8 0.0 collective-permute-done.4.refs_1_.refs_16_
  19.9 0.0 copy-done
  19.9 2.3 %pick.1 = (bf16[40,16,128]{2,1,0:T(8,128)(2,1)S(1)}, bf16[68,16,128]{2,1,0:T(8,128)(2,1)S(1)}, bf16[40,16,128]{2,1,0:T(8,128)(2,1)S(1)}, bf16[44,16,128]{2,1,0:T...) custom-call(s32[8,128]{1,0:T(8,128)S(1)} %bitcast.10, ...), custom_call_target="tpu_custom_call" | custom-call | tf_op jit(solution)/shard_map/pick/pallas_call | solution.py:298
  22.2 0.6 collective-permute-start.8
  22.8 0.7 while.15
  23.4 0.6 collective-permute-start.11
  24.1 3.3 %collective-permute-start.12 = (bf16[28,16,128]{2,1,0:T(8,128)(2,1)S(1)}, bf16[28,16,128]{2,1,0:T(8,128)(2,1)S(1)}, u32[]{:S(2)}, u32[]{:S(2)}) collective-permute-start(bf16[28,16,128]{2,1,0:T(8,128)(2,1)S(1)} %get-tuple-element.72), channel_id=1, source_target_pairs={{0,5},{1,4},{2,7},{3,6},{4,1},{5,0},{6,3},{7,2},{8,13},{9,12},{10,... | collective-permute-start | bytes 344072 | tf_op jit(solution)/shard_map/ppermute | solution.py:662
  27.4 0.5 collective-permute-start.10
  27.9 1.4 %collective-permute-start.9 = (bf16[40,16,128]{2,1,0:T(8,128)(2,1)S(1)}, bf16[40,16,128]{2,1,0:T(8,128)(2,1)S(1)}, u32[]{:S(2)}, u32[]{:S(2)}) collective-permute-start(bf16[40,16,128]{2,1,0:T(8,128)(2,1)S(1)} %get-tuple-element.69), channel_id=1, source_target_pairs={{0,2},{1,3},{2,0},{3,1},{4,6},{5,7},{6,4},{7,5},{8,10},{9,11},{10,... | collective-permute-start | bytes 491528 | tf_op jit(solution)/shard_map/ppermute | solution.py:662
  29.4 3.4 %collective-permute-done.11.refs_7_ = bf16[28,16,128]{2,1,0:T(8,128)(2,1)S(1)} collective-permute-done((bf16[28,16,128]{2,1,0:T(8,128)(2,1)S(1)}, bf16[28,16,128]{2,1,0:T(8,128)(2,1)S(1)}, u32[]{:S(2)}, u32[]{:S(2)}) %collective-permute-start.11) | collective-permute-done | bytes 114720 | tf_op jit(solution)/shard_map/ppermute | solution.py:662
  32.8 2.6 %collective-permute-start.14 = (bf16[32,16,128]{2,1,0:T(8,128)(2,1)S(1)}, bf16[32,16,128]{2,1,0:T(8,128)(2,1)S(1)}, u32[]{:S(2)}, u32[]{:S(2)}) collective-permute-start(bf16[32,16,128]{2,1,0:T(8,128)(2,1)S(1)} %get-tuple-element.74), channel_id=1, source_target_pairs={{0,7},{1,6},{2,5},{3,4},{4,3},{5,2},{6,1},{7,0},{8,15},{9,14},{10,... | collective-permute-start | bytes 393224 | tf_op jit(solution)/shard_map/ppermute | solution.py:662
  35.4 0.8 %collective-permute-done.12.refs_8_ = bf16[28,16,128]{2,1,0:T(8,128)(2,1)S(1)} collective-permute-done((bf16[28,16,128]{2,1,0:T(8,128)(2,1)S(1)}, bf16[28,16,128]{2,1,0:T(8,128)(2,1)S(1)}, u32[]{:S(2)}, u32[]{:S(2)}) %collective-permute-start.12) | collective-permute-done | bytes 114720 | tf_op jit(solution)/shard_map/ppermute | solution.py:662
  36.3 1.5 %collective-permute-start.13 = (bf16[28,16,128]{2,1,0:T(8,128)(2,1)S(1)}, bf16[28,16,128]{2,1,0:T(8,128)(2,1)S(1)}, u32[]{:S(2)}, u32[]{:S(2)}) collective-permute-start(bf16[28,16,128]{2,1,0:T(8,128)(2,1)S(1)} %get-tuple-element.73), channel_id=1, source_target_pairs={{0,6},{1,7},{2,4},{3,5},{4,2},{5,3},{6,0},{7,1},{8,14},{9,15},{10,... | collective-permute-start | bytes 344072 | tf_op jit(solution)/shard_map/ppermute | solution.py:662
  37.8 5.2 %collective-permute-done.13.refs_9_ = bf16[28,16,128]{2,1,0:T(8,128)(2,1)S(1)} collective-permute-done((bf16[28,16,128]{2,1,0:T(8,128)(2,1)S(1)}, bf16[28,16,128]{2,1,0:T(8,128)(2,1)S(1)}, u32[]{:S(2)}, u32[]{:S(2)}) %collective-permute-start.13) | collective-permute-done | bytes 114720 | tf_op jit(solution)/shard_map/ppermute | solution.py:662
  43.0 0.0 collective-permute-done.14.refs_10_
  43.0 2.0 %collective-permute-done.9.refs_5_ = bf16[40,16,128]{2,1,0:T(8,128)(2,1)S(1)} collective-permute-done((bf16[40,16,128]{2,1,0:T(8,128)(2,1)S(1)}, bf16[40,16,128]{2,1,0:T(8,128)(2,1)S(1)}, u32[]{:S(2)}, u32[]{:S(2)}) %collective-permute-start.9) | collective-permute-done | bytes 163872 | tf_op jit(solution)/shard_map/ppermute | solution.py:662
  45.0 0.0 collective-permute-done.10.refs_6_
  45.0 0.0 collective-permute-done.8.refs_4_
  45.0 0.0 copy-done.1
  45.0 7.2 %first.1 = (f32[2,68,16,128]{3,2,1,0:T(8,128)S(1)}, f32[3,2,68,16,128]{4,3,2,1,0:T(8,128)S(1)}, f32[2,68,16,128]{3,2,1,0:T(8,128)S(1)}, f32[3,2,66,16,128]{4,3,2...) custom-call(s32[1,2]{1,0:T(1,128)S(1)} %bitcast.14, s32[2,64]{1,0:T(2,128)S(1)} %get-tuple-element.61.refs_1_, ...), custom_call_target="tpu_custom_call" | custom-call | tf_op jit(solution)/shard_map/first/pallas_call | solution.py:524
  52.2 0.1 collective-permute-start.15
  52.3 1.5 %collective-permute-done.15 = f32[66,8,128]{2,1,0:T(8,128)S(1)} collective-permute-done((f32[66,8,128]{2,1,0:T(8,128)S(1)}, f32[66,8,128]{2,1,0:T(8,128)S(1)}, u32[]{:S(2)}, u32[]{:S(2)}) %collective-permute-start.15) | collective-permute-done | bytes 270368 | tf_op jit(solution)/shard_map/ppermute | solution.py:662
  53.8 0.1 fusion
  53.9 1.5 %collective-permute-start.16 = (bf16[66,8,128]{2,1,0:T(8,128)(2,1)S(1)}, bf16[66,8,128]{2,1,0:T(8,128)(2,1)S(1)}, u32[]{:S(2)}, u32[]{:S(2)}) collective-permute-start(bf16[66,8,128]{2,1,0:T(8,128)(2,1)S(1)} %get-tuple-element.105), channel_id=1, source_target_pairs={{0,16},{8,24},{16,0},{24,8},{1,17},{9,25},{17,1},{25,9},{2,18},{10... | collective-permute-start | bytes 405512 | tf_op jit(solution)/shard_map/ppermute | solution.py:662
  55.4 4.2 %collective-permute-done.16 = bf16[66,8,128]{2,1,0:T(8,128)(2,1)S(1)} collective-permute-done((bf16[66,8,128]{2,1,0:T(8,128)(2,1)S(1)}, bf16[66,8,128]{2,1,0:T(8,128)(2,1)S(1)}, u32[]{:S(2)}, u32[]{:S(2)}) %collective-permute-start.16) | collective-permute-done | bytes 135200 | tf_op jit(solution)/shard_map/ppermute | solution.py:662
  59.6 0.1 collective-permute-start.17
  59.7 1.3 %collective-permute-done.17.other_ref = bf16[66,8,128]{2,1,0:T(8,128)(2,1)S(1)} collective-permute-done((bf16[66,8,128]{2,1,0:T(8,128)(2,1)S(1)}, bf16[66,8,128]{2,1,0:T(8,128)(2,1)S(1)}, u32[]{:S(2)}, u32[]{:S(2)}) %collective-permute-start.17) | collective-permute-done | bytes 135200 | tf_op jit(solution)/shard_map/ppermute | solution.py:662
  61.1 3.2 %last.1 = (f32[3,2,64,16,128]{4,3,2,1,0:T(8,128)}, f32[64,8,128]{2,1,0:T(8,128)S(1)}, f32[64,8,128]{2,1,0:T(8,128)S(1)}) custom-call(bf16[66,8,128]{2,1,0:T(8,128)(2,1)S(1)} %multiply_convert_fusion.mine_ref, bf16[66,8,128]{2,1,0:T(8,128)(2,1)S(1)} %collective-permute-done.17.other_ref, f32[2,68,16,128]{3,2,1,0:T(8,128)S(1)} %get-tuple-element.86.warped_ref, ...), custom_call_target="tpu_custom_call" | custom-call | tf_op jit(solution)/shard_map/last/pallas_call | solution.py:618
  64.3 0.2 collective-permute-start.18
  64.5 1.4 %collective-permute-done.18.got_ref = f32[64,8,128]{2,1,0:T(8,128)S(1)} collective-permute-done((f32[64,8,128]{2,1,0:T(8,128)S(1)}, f32[64,8,128]{2,1,0:T(8,128)S(1)}, u32[]{:S(2)}, u32[]{:S(2)}) %collective-permute-start.18) | collective-permute-done | bytes 262176 | tf_op jit(solution)/shard_map/ppermute | solution.py:662
  65.9 0.1 fold.1
  66.0 1.5 %collective-permute-start.19 = (f32[64,4,128]{2,1,0:T(4,128)S(1)}, f32[64,4,128]{2,1,0:T(4,128)S(1)}, u32[]{:S(2)}, u32[]{:S(2)}) collective-permute-start(f32[64,4,128]{2,1,0:T(4,128)S(1)} %get-tuple-element.94), channel_id=1, source_target_pairs={{0,16},{8,24},{16,0},{24,8},{1,17},{9,25},{17,1},{25,9},{2,18},{10... | collective-permute-start | bytes 393224 | tf_op jit(solution)/shard_map/ppermute | solution.py:662
  67.4 4.1 %collective-permute-done.19 = f32[64,4,128]{2,1,0:T(4,128)S(1)} collective-permute-done((f32[64,4,128]{2,1,0:T(4,128)S(1)}, f32[64,4,128]{2,1,0:T(4,128)S(1)}, u32[]{:S(2)}, u32[]{:S(2)}) %collective-permute-start.19) | collective-permute-done | bytes 131104 | tf_op jit(solution)/shard_map/ppermute | solution.py:662
  71.6 0.7 add_multiply_fusion
  (1 shorter events, 0.0 us)
Async XLA Ops:
  0.6 19.2 %copy-start = (f32[64,4,128]{2,1,0:T(4,128)S(1)}, f32[64,4,128]{2,1,0:T(4,128)}, u32[]{:S(2)}) copy-start(f32[64,4,128]{2,1,0:T(4,128)} %refs_15_.1) | copy-start | bytes 393220
  0.6 19.2 %collective-permute-start.6 = (f32[64,4,128]{2,1,0:T(4,128)}, f32[64,4,128]{2,1,0:T(4,128)S(1)}, u32[]{:S(2)}, u32[]{:S(2)}) collective-permute-start(f32[64,4,128]{2,1,0:T(4,128)} %refs_15_.1), channel_id=1, source_target_pairs={{0,24},{8,16},{16,8},{24,0},{1,25},{9,17},{17,9},{25,1},{2,26},{10... | collective-permute-start | bytes 393224 | tf_op jit(solution)/shard_map/ppermute | solution.py:662
  3.1 16.8 %collective-permute-start.5 = (f32[64,4,128]{2,1,0:T(4,128)}, f32[64,4,128]{2,1,0:T(4,128)S(1)}, u32[]{:S(2)}, u32[]{:S(2)}) collective-permute-start(f32[64,4,128]{2,1,0:T(4,128)} %refs_15_.1), channel_id=1, source_target_pairs={{0,16},{8,24},{16,0},{24,8},{1,17},{9,25},{17,1},{25,9},{2,18},{10... | collective-permute-start | bytes 393224 | tf_op jit(solution)/shard_map/ppermute | solution.py:662
  3.7 16.1 %collective-permute-start.4 = (f32[64,4,128]{2,1,0:T(4,128)}, f32[64,4,128]{2,1,0:T(4,128)S(1)}, u32[]{:S(2)}, u32[]{:S(2)}) collective-permute-start(f32[64,4,128]{2,1,0:T(4,128)} %refs_15_.1), channel_id=1, source_target_pairs={{0,8},{8,0},{16,24},{24,16},{1,9},{9,1},{17,25},{25,17},{2,10},{10... | collective-permute-start | bytes 393224 | tf_op jit(solution)/shard_map/ppermute | solution.py:662
  3.8 41.2 %copy-start.1 = (s32[2,1]{0,1:T(1,128)S(1)}, s32[2,1]{0,1:T(1,128)}, u32[]{:S(2)}) copy-start(s32[2,1]{0,1:T(1,128)} %param.15) | copy-start | bytes 28
  5.1 14.8 %collective-permute-start.7 = (bf16[24,16,128]{2,1,0:T(8,128)(2,1)S(1)}, bf16[24,16,128]{2,1,0:T(8,128)(2,1)S(1)}, u32[]{:S(2)}, u32[]{:S(2)}) collective-permute-start(bf16[24,16,128]{2,1,0:T(8,128)(2,1)S(1)} %get-tuple-element.65), channel_id=1, source_target_pairs={{1,2},{3,4},{5,6},{2,1},{4,3},{6,5},{9,10},{11,12},{13,14},{10,9},... | collective-permute-start | bytes 294920 | tf_op jit(solution)/shard_map/ppermute | solution.py:684
  22.2 22.8 %collective-permute-start.8 = (bf16[68,16,128]{2,1,0:T(8,128)(2,1)S(1)}, bf16[68,16,128]{2,1,0:T(8,128)(2,1)S(1)}, u32[]{:S(2)}, u32[]{:S(2)}) collective-permute-start(bf16[68,16,128]{2,1,0:T(8,128)(2,1)S(1)} %get-tuple-element.68), channel_id=1, source_target_pairs={{0,1},{1,0},{2,3},{3,2},{4,5},{5,4},{6,7},{7,6},{8,9},{9,8},{10,11... | collective-permute-start | bytes 835592 | tf_op jit(solution)/shard_map/ppermute | solution.py:662
  23.4 9.4 %collective-permute-start.11 = (bf16[28,16,128]{2,1,0:T(8,128)(2,1)S(1)}, bf16[28,16,128]{2,1,0:T(8,128)(2,1)S(1)}, u32[]{:S(2)}, u32[]{:S(2)}) collective-permute-start(bf16[28,16,128]{2,1,0:T(8,128)(2,1)S(1)} %get-tuple-element.71), channel_id=1, source_target_pairs={{0,4},{1,5},{2,6},{3,7},{4,0},{5,1},{6,2},{7,3},{8,12},{9,13},{10,... | collective-permute-start | bytes 344072 | tf_op jit(solution)/shard_map/ppermute | solution.py:662
  24.1 12.2 %collective-permute-start.12 = (bf16[28,16,128]{2,1,0:T(8,128)(2,1)S(1)}, bf16[28,16,128]{2,1,0:T(8,128)(2,1)S(1)}, u32[]{:S(2)}, u32[]{:S(2)}) collective-permute-start(bf16[28,16,128]{2,1,0:T(8,128)(2,1)S(1)} %get-tuple-element.72), channel_id=1, source_target_pairs={{0,5},{1,4},{2,7},{3,6},{4,1},{5,0},{6,3},{7,2},{8,13},{9,12},{10,... | collective-permute-start | bytes 344072 | tf_op jit(solution)/shard_map/ppermute | solution.py:662
  27.4 17.6 %collective-permute-start.10 = (bf16[44,16,128]{2,1,0:T(8,128)(2,1)S(1)}, bf16[44,16,128]{2,1,0:T(8,128)(2,1)S(1)}, u32[]{:S(2)}, u32[]{:S(2)}) collective-permute-start(bf16[44,16,128]{2,1,0:T(8,128)(2,1)S(1)} %get-tuple-element.70), channel_id=1, source_target_pairs={{0,3},{1,2},{2,1},{3,0},{4,7},{5,6},{6,5},{7,4},{8,11},{9,10},{10,... | collective-permute-start | bytes 540680 | tf_op jit(solution)/shard_map/ppermute | solution.py:662
  27.9 17.1 %collective-permute-start.9 = (bf16[40,16,128]{2,1,0:T(8,128)(2,1)S(1)}, bf16[40,16,128]{2,1,0:T(8,128)(2,1)S(1)}, u32[]{:S(2)}, u32[]{:S(2)}) collective-permute-start(bf16[40,16,128]{2,1,0:T(8,128)(2,1)S(1)} %get-tuple-element.69), channel_id=1, source_target_pairs={{0,2},{1,3},{2,0},{3,1},{4,6},{5,7},{6,4},{7,5},{8,10},{9,11},{10,... | collective-permute-start | bytes 491528 | tf_op jit(solution)/shard_map/ppermute | solution.py:662
  32.8 10.3 %collective-permute-start.14 = (bf16[32,16,128]{2,1,0:T(8,128)(2,1)S(1)}, bf16[32,16,128]{2,1,0:T(8,128)(2,1)S(1)}, u32[]{:S(2)}, u32[]{:S(2)}) collective-permute-start(bf16[32,16,128]{2,1,0:T(8,128)(2,1)S(1)} %get-tuple-element.74), channel_id=1, source_target_pairs={{0,7},{1,6},{2,5},{3,4},{4,3},{5,2},{6,1},{7,0},{8,15},{9,14},{10,... | collective-permute-start | bytes 393224 | tf_op jit(solution)/shard_map/ppermute | solution.py:662
  36.3 6.8 %collective-permute-start.13 = (bf16[28,16,128]{2,1,0:T(8,128)(2,1)S(1)}, bf16[28,16,128]{2,1,0:T(8,128)(2,1)S(1)}, u32[]{:S(2)}, u32[]{:S(2)}) collective-permute-start(bf16[28,16,128]{2,1,0:T(8,128)(2,1)S(1)} %get-tuple-element.73), channel_id=1, source_target_pairs={{0,6},{1,7},{2,4},{3,5},{4,2},{5,3},{6,0},{7,1},{8,14},{9,15},{10,... | collective-permute-start | bytes 344072 | tf_op jit(solution)/shard_map/ppermute | solution.py:662
  52.2 1.6 %collective-permute-start.15 = (f32[66,8,128]{2,1,0:T(8,128)S(1)}, f32[66,8,128]{2,1,0:T(8,128)S(1)}, u32[]{:S(2)}, u32[]{:S(2)}) collective-permute-start(f32[66,8,128]{2,1,0:T(8,128)S(1)} %get-tuple-element.85), channel_id=1, source_target_pairs={{0,8},{8,0},{16,24},{24,16},{1,9},{9,1},{17,25},{25,17},{2,10},{10... | collective-permute-start | bytes 811016 | tf_op jit(solution)/shard_map/ppermute | solution.py:662
  53.9 5.7 %collective-permute-start.16 = (bf16[66,8,128]{2,1,0:T(8,128)(2,1)S(1)}, bf16[66,8,128]{2,1,0:T(8,128)(2,1)S(1)}, u32[]{:S(2)}, u32[]{:S(2)}) collective-permute-start(bf16[66,8,128]{2,1,0:T(8,128)(2,1)S(1)} %get-tuple-element.105), channel_id=1, source_target_pairs={{0,16},{8,24},{16,0},{24,8},{1,17},{9,25},{17,1},{25,9},{2,18},{10... | collective-permute-start | bytes 405512 | tf_op jit(solution)/shard_map/ppermute | solution.py:662
  59.6 1.4 %collective-permute-start.17 = (bf16[66,8,128]{2,1,0:T(8,128)(2,1)S(1)}, bf16[66,8,128]{2,1,0:T(8,128)(2,1)S(1)}, u32[]{:S(2)}, u32[]{:S(2)}) collective-permute-start(bf16[66,8,128]{2,1,0:T(8,128)(2,1)S(1)} %multiply_convert_fusion.mine_ref), channel_id=1, source_target_pairs={{0,8},{8,0},{16,24},{24,16},{1,9},{9,1},{17,25},{25,17},{2,10},{10... | collective-permute-start | bytes 405512 | tf_op jit(solution)/shard_map/ppermute | solution.py:662
  64.3 1.6 %collective-permute-start.18 = (f32[64,8,128]{2,1,0:T(8,128)S(1)}, f32[64,8,128]{2,1,0:T(8,128)S(1)}, u32[]{:S(2)}, u32[]{:S(2)}) collective-permute-start(f32[64,8,128]{2,1,0:T(8,128)S(1)} %get-tuple-element.92), channel_id=1, source_target_pairs={{0,8},{8,0},{16,24},{24,16},{1,9},{9,1},{17,25},{25,17},{2,10},{10... | collective-permute-start | bytes 786440 | tf_op jit(solution)/shard_map/ppermute | solution.py:662
  66.0 5.6 %collective-permute-start.19 = (f32[64,4,128]{2,1,0:T(4,128)S(1)}, f32[64,4,128]{2,1,0:T(4,128)S(1)}, u32[]{:S(2)}, u32[]{:S(2)}) collective-permute-start(f32[64,4,128]{2,1,0:T(4,128)S(1)} %get-tuple-element.94), channel_id=1, source_target_pairs={{0,16},{8,24},{16,0},{24,8},{1,17},{9,25},{17,1},{25,9},{2,18},{10... | collective-permute-start | bytes 393224 | tf_op jit(solution)/shard_map/ppermute | solution.py:662

commit v2 on v1

--- a/solution.py
+++ b/solution.py
@@ -8,7 +8,6 @@
 from jax.sharding import PartitionSpec as P
 
 BY = 4
-ITERS = 2
 RIDGE = 0.25
 LANES = 128
 LIMIT = 24 * 1024 * 1024
@@ -511,7 +510,7 @@
         send_ref[i] = jnp.where(core == 0, high, low)
         return carry
 
-    lax.fori_loop(0, rows + 2, move, 0, unroll=11)
+    lax.fori_loop(0, rows + 2, move, 0, unroll=22)
 
 
 def first(counts, slots, edge_slots, parts, overs, shares, side, weights, velocity):
@@ -538,7 +537,7 @@
             pltpu.VMEM((3, subj_dev, long, plane, depth), jnp.float32),
             pltpu.VMEM(weights.shape, weights.dtype),
             pltpu.VMEM((2, side.shape[0] + 2 * EDGE) + side.shape[1:], side.dtype),
-            pltpu.SemaphoreType.DMA((8,)),
+            pltpu.SemaphoreType.DMA((16,)),
         ],
         compiler_params=params(),
         name="first",
@@ -578,7 +577,7 @@
                 update[c, s, i] = g[c] * ratio
         return carry
 
-    lax.fori_loop(0, rows + 2, renew, 0, unroll=11)
+    lax.fori_loop(0, rows + 2, renew, 0, unroll=22)
 
     def move(r, carry):
         total = None
@@ -602,7 +601,7 @@
 
     copies = []
     for i in range(chunks):
-        lax.fori_loop(i * chunk, (i + 1) * chunk, move, 0, unroll=16)
+        lax.fori_loop(i * chunk, (i + 1) * chunk, move, 0, unroll=8)
         part = pl.ds(i * chunk, chunk)
         copy = pltpu.make_async_copy(out.at[:, :, part], out_ref.at[:, :, part], sems.at[i])
         copy.start()
@@ -623,7 +622,7 @@
         scratch_shapes=[
             pltpu.VMEM(field.shape, jnp.float32),
             pltpu.VMEM(shape, jnp.float32),
-            pltpu.SemaphoreType.DMA((4,)),
+            pltpu.SemaphoreType.DMA((8,)),
         ],
         compiler_params=params(),
         name="last",

time: 72.5 us -> 72.1 us (level)
  no operation moved by 1% of the time
where the time goes in v2:
time: 72.1 us; the launch traced here: 71.9 us
  waiting for transfers between devices  24.3 us (34%)
  starting transfers between devices  17.6 us (24%)
  blocking collectives  14.1 us (20%)
  Pallas kernels  13.6 us (19%)
  other arithmetic  0.81 us (1%)
  between operations  0.75 us (1%)
    ppermute x15, waiting for transfers between devices, swap(): return lax.ppermute(value, axis, [(i, i ^ mask) for i in range(count)])  24.3 us
    ppermute x15, starting transfers between devices, swap(): return lax.ppermute(value, axis, [(i, i ^ mask) for i in range(count)])  16.9 us
    all_to_all x1, blocking collectives, body(): lax.all_to_all(request, 'space', split_axis=0, concat_axis=0, tiled=True)  14.1 us
    pallas_call x1, Pallas kernels, first(): pl.pallas_call(functools.partial(first_kernel, spaces, spaces - len(overs...  6.93 us
    pallas_call x1, Pallas kernels, last(): pl.pallas_call(last_kernel, out_shape=(shaped(shape), sums, sums), in_spe...  3.09 us
    pallas_call x1, Pallas kernels, pick(): pl.pallas_call(functools.partial(pick_kernel, cap, base, total, len(share...  2.27 us
  transfers between devices with their start and end apart: 16, of which 9 were waited for; matrix products, arithmetic and copies ran while one was open for 0% of the time, Pallas kernels for 2%

profile of v2, /device:TPU:0, one launch (start us, length us, event | category | flops | bytes accessed | tf_op | source)
XLA Modules:
  0.0 71.9 jit_solution(14511302613034212635)
XLA Ops:
  0.6 0.0 copy-start
  0.6 2.4 %collective-permute-start.6 = (f32[64,4,128]{2,1,0:T(4,128)}, f32[64,4,128]{2,1,0:T(4,128)S(1)}, u32[]{:S(2)}, u32[]{:S(2)}) collective-permute-start(f32[64,4,128]{2,1,0:T(4,128)} %refs_15_.1), channel_id=1, source_target_pairs={{0,24},{8,16},{16,8},{24,0},{1,25},{9,17},{17,9},{25,1},{2,26},{10... | collective-permute-start | bytes 393224 | tf_op jit(solution)/shard_map/ppermute | solution.py:661
  3.1 0.6 collective-permute-start.5
  3.7 0.0 collective-permute-start.4
  3.8 0.0 copy-start.1
  3.8 1.3 %plan.1 = (s32[8,128]{1,0:T(8,128)S(1)}, s32[2,64]{1,0:T(2,128)S(1)}, bf16[128,16,128]{2,1,0:T(8,128)(2,1)S(1)}, bf16[24,16,128]{2,1,0:T(8,128)(2,1)S(1)}, bf16[24,16,128]{2,1,0:T(8,128)(2,1)S(1)}) custom-call(s32[1,2]{1,0:T(1,128)} %bitcast.13, s32[2,1,64]{2,1,0:T(1,128)} %bitcast.16, s32[2,64]{1,0:T(2,128)} %rows_in.1, bf16[128,16,128]{2,1,0:T(8,128)(2,1)} %bitcast.15, ...), custom_call_target="tpu_custom_call" | custom-call | tf_op jit(solution)/shard_map/plan/pallas_call | solution.py:158
  5.1 0.7 collective-permute-start.7
  5.7 14.1 %all_to_all.11 = s32[8,1,128]{2,1,0:T(1,128)S(1)} all-to-all(s32[8,1,128]{2,1,0:T(1,128)S(1)} %bitcast.12), channel_id=1, replica_groups=mesh['subj'=4,'space'=8] {'space'}, dimensions={0} | all-to-all | bytes 8192 | tf_op jit(solution)/shard_map/all_to_all | solution.py:685
  19.8 0.0 collective-permute-done.7.refs_4_.refs_19_
  19.8 0.0 collective-permute-done.6.refs_3_.refs_18_
  19.8 0.0 collective-permute-done.5.refs_2_.refs_17_
  19.8 0.0 collective-permute-done.4.refs_1_.refs_16_
  19.9 0.0 copy-done
  19.9 2.3 %pick.1 = (bf16[40,16,128]{2,1,0:T(8,128)(2,1)S(1)}, bf16[68,16,128]{2,1,0:T(8,128)(2,1)S(1)}, bf16[40,16,128]{2,1,0:T(8,128)(2,1)S(1)}, bf16[44,16,128]{2,1,0:T...) custom-call(s32[8,128]{1,0:T(8,128)S(1)} %bitcast.10, ...), custom_call_target="tpu_custom_call" | custom-call | tf_op jit(solution)/shard_map/pick/pallas_call | solution.py:297
  22.1 0.6 collective-permute-start.8
  22.8 0.7 while.15
  23.4 0.6 collective-permute-start.11
  24.1 3.3 %collective-permute-start.12 = (bf16[28,16,128]{2,1,0:T(8,128)(2,1)S(1)}, bf16[28,16,128]{2,1,0:T(8,128)(2,1)S(1)}, u32[]{:S(2)}, u32[]{:S(2)}) collective-permute-start(bf16[28,16,128]{2,1,0:T(8,128)(2,1)S(1)} %get-tuple-element.72), channel_id=1, source_target_pairs={{0,5},{1,4},{2,7},{3,6},{4,1},{5,0},{6,3},{7,2},{8,13},{9,12},{10,... | collective-permute-start | bytes 344072 | tf_op jit(solution)/shard_map/ppermute | solution.py:661
  27.3 0.6 collective-permute-start.10
  27.9 1.4 %collective-permute-start.9 = (bf16[40,16,128]{2,1,0:T(8,128)(2,1)S(1)}, bf16[40,16,128]{2,1,0:T(8,128)(2,1)S(1)}, u32[]{:S(2)}, u32[]{:S(2)}) collective-permute-start(bf16[40,16,128]{2,1,0:T(8,128)(2,1)S(1)} %get-tuple-element.69), channel_id=1, source_target_pairs={{0,2},{1,3},{2,0},{3,1},{4,6},{5,7},{6,4},{7,5},{8,10},{9,11},{10,... | collective-permute-start | bytes 491528 | tf_op jit(solution)/shard_map/ppermute | solution.py:661
  29.3 3.4 %collective-permute-done.11.refs_7_ = bf16[28,16,128]{2,1,0:T(8,128)(2,1)S(1)} collective-permute-done((bf16[28,16,128]{2,1,0:T(8,128)(2,1)S(1)}, bf16[28,16,128]{2,1,0:T(8,128)(2,1)S(1)}, u32[]{:S(2)}, u32[]{:S(2)}) %collective-permute-start.11) | collective-permute-done | bytes 114720 | tf_op jit(solution)/shard_map/ppermute | solution.py:661
  32.8 2.6 %collective-permute-start.14 = (bf16[32,16,128]{2,1,0:T(8,128)(2,1)S(1)}, bf16[32,16,128]{2,1,0:T(8,128)(2,1)S(1)}, u32[]{:S(2)}, u32[]{:S(2)}) collective-permute-start(bf16[32,16,128]{2,1,0:T(8,128)(2,1)S(1)} %get-tuple-element.74), channel_id=1, source_target_pairs={{0,7},{1,6},{2,5},{3,4},{4,3},{5,2},{6,1},{7,0},{8,15},{9,14},{10,... | collective-permute-start | bytes 393224 | tf_op jit(solution)/shard_map/ppermute | solution.py:661
  35.4 0.9 %collective-permute-done.12.refs_8_ = bf16[28,16,128]{2,1,0:T(8,128)(2,1)S(1)} collective-permute-done((bf16[28,16,128]{2,1,0:T(8,128)(2,1)S(1)}, bf16[28,16,128]{2,1,0:T(8,128)(2,1)S(1)}, u32[]{:S(2)}, u32[]{:S(2)}) %collective-permute-start.12) | collective-permute-done | bytes 114720 | tf_op jit(solution)/shard_map/ppermute | solution.py:661
  36.2 1.5 %collective-permute-start.13 = (bf16[28,16,128]{2,1,0:T(8,128)(2,1)S(1)}, bf16[28,16,128]{2,1,0:T(8,128)(2,1)S(1)}, u32[]{:S(2)}, u32[]{:S(2)}) collective-permute-start(bf16[28,16,128]{2,1,0:T(8,128)(2,1)S(1)} %get-tuple-element.73), channel_id=1, source_target_pairs={{0,6},{1,7},{2,4},{3,5},{4,2},{5,3},{6,0},{7,1},{8,14},{9,15},{10,... | collective-permute-start | bytes 344072 | tf_op jit(solution)/shard_map/ppermute | solution.py:661
  37.7 5.2 %collective-permute-done.13.refs_9_ = bf16[28,16,128]{2,1,0:T(8,128)(2,1)S(1)} collective-permute-done((bf16[28,16,128]{2,1,0:T(8,128)(2,1)S(1)}, bf16[28,16,128]{2,1,0:T(8,128)(2,1)S(1)}, u32[]{:S(2)}, u32[]{:S(2)}) %collective-permute-start.13) | collective-permute-done | bytes 114720 | tf_op jit(solution)/shard_map/ppermute | solution.py:661
  42.9 0.0 collective-permute-done.14.refs_10_
  42.9 2.1 %collective-permute-done.9.refs_5_ = bf16[40,16,128]{2,1,0:T(8,128)(2,1)S(1)} collective-permute-done((bf16[40,16,128]{2,1,0:T(8,128)(2,1)S(1)}, bf16[40,16,128]{2,1,0:T(8,128)(2,1)S(1)}, u32[]{:S(2)}, u32[]{:S(2)}) %collective-permute-start.9) | collective-permute-done | bytes 163872 | tf_op jit(solution)/shard_map/ppermute | solution.py:661
  45.0 0.0 collective-permute-done.10.refs_6_
  45.0 0.0 collective-permute-done.8.refs_4_
  45.0 0.0 copy-done.1
  45.0 6.9 %first.1 = (f32[2,68,16,128]{3,2,1,0:T(8,128)S(1)}, f32[3,2,68,16,128]{4,3,2,1,0:T(8,128)S(1)}, f32[2,68,16,128]{3,2,1,0:T(8,128)S(1)}, f32[3,2,66,16,128]{4,3,2...) custom-call(s32[1,2]{1,0:T(1,128)S(1)} %bitcast.14, s32[2,64]{1,0:T(2,128)S(1)} %get-tuple-element.61.refs_1_, ...), custom_call_target="tpu_custom_call" | custom-call | tf_op jit(solution)/shard_map/first/pallas_call | solution.py:523
  52.0 0.1 collective-permute-start.15
  52.0 1.5 %collective-permute-done.15 = f32[66,8,128]{2,1,0:T(8,128)S(1)} collective-permute-done((f32[66,8,128]{2,1,0:T(8,128)S(1)}, f32[66,8,128]{2,1,0:T(8,128)S(1)}, u32[]{:S(2)}, u32[]{:S(2)}) %collective-permute-start.15) | collective-permute-done | bytes 270368 | tf_op jit(solution)/shard_map/ppermute | solution.py:661
  53.6 0.1 fusion
  53.6 1.4 %collective-permute-start.16 = (bf16[66,8,128]{2,1,0:T(8,128)(2,1)S(1)}, bf16[66,8,128]{2,1,0:T(8,128)(2,1)S(1)}, u32[]{:S(2)}, u32[]{:S(2)}) collective-permute-start(bf16[66,8,128]{2,1,0:T(8,128)(2,1)S(1)} %get-tuple-element.105), channel_id=1, source_target_pairs={{0,16},{8,24},{16,0},{24,8},{1,17},{9,25},{17,1},{25,9},{2,18},{10... | collective-permute-start | bytes 405512 | tf_op jit(solution)/shard_map/ppermute | solution.py:661
  55.1 4.3 %collective-permute-done.16 = bf16[66,8,128]{2,1,0:T(8,128)(2,1)S(1)} collective-permute-done((bf16[66,8,128]{2,1,0:T(8,128)(2,1)S(1)}, bf16[66,8,128]{2,1,0:T(8,128)(2,1)S(1)}, u32[]{:S(2)}, u32[]{:S(2)}) %collective-permute-start.16) | collective-permute-done | bytes 135200 | tf_op jit(solution)/shard_map/ppermute | solution.py:661
  59.4 0.1 collective-permute-start.17
  59.4 1.3 %collective-permute-done.17.other_ref = bf16[66,8,128]{2,1,0:T(8,128)(2,1)S(1)} collective-permute-done((bf16[66,8,128]{2,1,0:T(8,128)(2,1)S(1)}, bf16[66,8,128]{2,1,0:T(8,128)(2,1)S(1)}, u32[]{:S(2)}, u32[]{:S(2)}) %collective-permute-start.17) | collective-permute-done | bytes 135200 | tf_op jit(solution)/shard_map/ppermute | solution.py:661
  60.8 3.1 %last.1 = (f32[3,2,64,16,128]{4,3,2,1,0:T(8,128)}, f32[64,8,128]{2,1,0:T(8,128)S(1)}, f32[64,8,128]{2,1,0:T(8,128)S(1)}) custom-call(bf16[66,8,128]{2,1,0:T(8,128)(2,1)S(1)} %multiply_convert_fusion.mine_ref, bf16[66,8,128]{2,1,0:T(8,128)(2,1)S(1)} %collective-permute-done.17.other_ref, f32[2,68,16,128]{3,2,1,0:T(8,128)S(1)} %get-tuple-element.86.warped_ref, ...), custom_call_target="tpu_custom_call" | custom-call | tf_op jit(solution)/shard_map/last/pallas_call | solution.py:617
  63.9 0.2 collective-permute-start.18
  64.1 1.4 %collective-permute-done.18.got_ref = f32[64,8,128]{2,1,0:T(8,128)S(1)} collective-permute-done((f32[64,8,128]{2,1,0:T(8,128)S(1)}, f32[64,8,128]{2,1,0:T(8,128)S(1)}, u32[]{:S(2)}, u32[]{:S(2)}) %collective-permute-start.18) | collective-permute-done | bytes 262176 | tf_op jit(solution)/shard_map/ppermute | solution.py:661
  65.5 0.1 fold.1
  65.6 1.4 %collective-permute-start.19 = (f32[64,4,128]{2,1,0:T(4,128)S(1)}, f32[64,4,128]{2,1,0:T(4,128)S(1)}, u32[]{:S(2)}, u32[]{:S(2)}) collective-permute-start(f32[64,4,128]{2,1,0:T(4,128)S(1)} %get-tuple-element.94), channel_id=1, source_target_pairs={{0,16},{8,24},{16,0},{24,8},{1,17},{9,25},{17,1},{25,9},{2,18},{10... | collective-permute-start | bytes 393224 | tf_op jit(solution)/shard_map/ppermute | solution.py:661
  67.0 4.2 %collective-permute-done.19 = f32[64,4,128]{2,1,0:T(4,128)S(1)} collective-permute-done((f32[64,4,128]{2,1,0:T(4,128)S(1)}, f32[64,4,128]{2,1,0:T(4,128)S(1)}, u32[]{:S(2)}, u32[]{:S(2)}) %collective-permute-start.19) | collective-permute-done | bytes 131104 | tf_op jit(solution)/shard_map/ppermute | solution.py:661
  71.2 0.7 add_multiply_fusion
  (1 shorter events, 0.0 us)
Async XLA Ops:
  0.6 19.2 %copy-start = (f32[64,4,128]{2,1,0:T(4,128)S(1)}, f32[64,4,128]{2,1,0:T(4,128)}, u32[]{:S(2)}) copy-start(f32[64,4,128]{2,1,0:T(4,128)} %refs_15_.1) | copy-start | bytes 393220
  0.6 19.2 %collective-permute-start.6 = (f32[64,4,128]{2,1,0:T(4,128)}, f32[64,4,128]{2,1,0:T(4,128)S(1)}, u32[]{:S(2)}, u32[]{:S(2)}) collective-permute-start(f32[64,4,128]{2,1,0:T(4,128)} %refs_15_.1), channel_id=1, source_target_pairs={{0,24},{8,16},{16,8},{24,0},{1,25},{9,17},{17,9},{25,1},{2,26},{10... | collective-permute-start | bytes 393224 | tf_op jit(solution)/shard_map/ppermute | solution.py:661
  3.1 16.8 %collective-permute-start.5 = (f32[64,4,128]{2,1,0:T(4,128)}, f32[64,4,128]{2,1,0:T(4,128)S(1)}, u32[]{:S(2)}, u32[]{:S(2)}) collective-permute-start(f32[64,4,128]{2,1,0:T(4,128)} %refs_15_.1), channel_id=1, source_target_pairs={{0,16},{8,24},{16,0},{24,8},{1,17},{9,25},{17,1},{25,9},{2,18},{10... | collective-permute-start | bytes 393224 | tf_op jit(solution)/shard_map/ppermute | solution.py:661
  3.7 16.1 %collective-permute-start.4 = (f32[64,4,128]{2,1,0:T(4,128)}, f32[64,4,128]{2,1,0:T(4,128)S(1)}, u32[]{:S(2)}, u32[]{:S(2)}) collective-permute-start(f32[64,4,128]{2,1,0:T(4,128)} %refs_15_.1), channel_id=1, source_target_pairs={{0,8},{8,0},{16,24},{24,16},{1,9},{9,1},{17,25},{25,17},{2,10},{10... | collective-permute-start | bytes 393224 | tf_op jit(solution)/shard_map/ppermute | solution.py:661
  3.8 41.2 %copy-start.1 = (s32[2,1]{0,1:T(1,128)S(1)}, s32[2,1]{0,1:T(1,128)}, u32[]{:S(2)}) copy-start(s32[2,1]{0,1:T(1,128)} %param.15) | copy-start | bytes 28
  5.1 14.8 %collective-permute-start.7 = (bf16[24,16,128]{2,1,0:T(8,128)(2,1)S(1)}, bf16[24,16,128]{2,1,0:T(8,128)(2,1)S(1)}, u32[]{:S(2)}, u32[]{:S(2)}) collective-permute-start(bf16[24,16,128]{2,1,0:T(8,128)(2,1)S(1)} %get-tuple-element.65), channel_id=1, source_target_pairs={{1,2},{3,4},{5,6},{2,1},{4,3},{6,5},{9,10},{11,12},{13,14},{10,9},... | collective-permute-start | bytes 294920 | tf_op jit(solution)/shard_map/ppermute | solution.py:683
  22.1 22.9 %collective-permute-start.8 = (bf16[68,16,128]{2,1,0:T(8,128)(2,1)S(1)}, bf16[68,16,128]{2,1,0:T(8,128)(2,1)S(1)}, u32[]{:S(2)}, u32[]{:S(2)}) collective-permute-start(bf16[68,16,128]{2,1,0:T(8,128)(2,1)S(1)} %get-tuple-element.68), channel_id=1, source_target_pairs={{0,1},{1,0},{2,3},{3,2},{4,5},{5,4},{6,7},{7,6},{8,9},{9,8},{10,11... | collective-permute-start | bytes 835592 | tf_op jit(solution)/shard_map/ppermute | solution.py:661
  23.4 9.3 %collective-permute-start.11 = (bf16[28,16,128]{2,1,0:T(8,128)(2,1)S(1)}, bf16[28,16,128]{2,1,0:T(8,128)(2,1)S(1)}, u32[]{:S(2)}, u32[]{:S(2)}) collective-permute-start(bf16[28,16,128]{2,1,0:T(8,128)(2,1)S(1)} %get-tuple-element.71), channel_id=1, source_target_pairs={{0,4},{1,5},{2,6},{3,7},{4,0},{5,1},{6,2},{7,3},{8,12},{9,13},{10,... | collective-permute-start | bytes 344072 | tf_op jit(solution)/shard_map/ppermute | solution.py:661
  24.1 12.2 %collective-permute-start.12 = (bf16[28,16,128]{2,1,0:T(8,128)(2,1)S(1)}, bf16[28,16,128]{2,1,0:T(8,128)(2,1)S(1)}, u32[]{:S(2)}, u32[]{:S(2)}) collective-permute-start(bf16[28,16,128]{2,1,0:T(8,128)(2,1)S(1)} %get-tuple-element.72), channel_id=1, source_target_pairs={{0,5},{1,4},{2,7},{3,6},{4,1},{5,0},{6,3},{7,2},{8,13},{9,12},{10,... | collective-permute-start | bytes 344072 | tf_op jit(solution)/shard_map/ppermute | solution.py:661
  27.3 17.7 %collective-permute-start.10 = (bf16[44,16,128]{2,1,0:T(8,128)(2,1)S(1)}, bf16[44,16,128]{2,1,0:T(8,128)(2,1)S(1)}, u32[]{:S(2)}, u32[]{:S(2)}) collective-permute-start(bf16[44,16,128]{2,1,0:T(8,128)(2,1)S(1)} %get-tuple-element.70), channel_id=1, source_target_pairs={{0,3},{1,2},{2,1},{3,0},{4,7},{5,6},{6,5},{7,4},{8,11},{9,10},{10,... | collective-permute-start | bytes 540680 | tf_op jit(solution)/shard_map/ppermute | solution.py:661
  27.9 17.1 %collective-permute-start.9 = (bf16[40,16,128]{2,1,0:T(8,128)(2,1)S(1)}, bf16[40,16,128]{2,1,0:T(8,128)(2,1)S(1)}, u32[]{:S(2)}, u32[]{:S(2)}) collective-permute-start(bf16[40,16,128]{2,1,0:T(8,128)(2,1)S(1)} %get-tuple-element.69), channel_id=1, source_target_pairs={{0,2},{1,3},{2,0},{3,1},{4,6},{5,7},{6,4},{7,5},{8,10},{9,11},{10,... | collective-permute-start | bytes 491528 | tf_op jit(solution)/shard_map/ppermute | solution.py:661
  32.8 10.1 %collective-permute-start.14 = (bf16[32,16,128]{2,1,0:T(8,128)(2,1)S(1)}, bf16[32,16,128]{2,1,0:T(8,128)(2,1)S(1)}, u32[]{:S(2)}, u32[]{:S(2)}) collective-permute-start(bf16[32,16,128]{2,1,0:T(8,128)(2,1)S(1)} %get-tuple-element.74), channel_id=1, source_target_pairs={{0,7},{1,6},{2,5},{3,4},{4,3},{5,2},{6,1},{7,0},{8,15},{9,14},{10,... | collective-permute-start | bytes 393224 | tf_op jit(solution)/shard_map/ppermute | solution.py:661
  36.2 6.7 %collective-permute-start.13 = (bf16[28,16,128]{2,1,0:T(8,128)(2,1)S(1)}, bf16[28,16,128]{2,1,0:T(8,128)(2,1)S(1)}, u32[]{:S(2)}, u32[]{:S(2)}) collective-permute-start(bf16[28,16,128]{2,1,0:T(8,128)(2,1)S(1)} %get-tuple-element.73), channel_id=1, source_target_pairs={{0,6},{1,7},{2,4},{3,5},{4,2},{5,3},{6,0},{7,1},{8,14},{9,15},{10,... | collective-permute-start | bytes 344072 | tf_op jit(solution)/shard_map/ppermute | solution.py:661
  52.0 1.6 %collective-permute-start.15 = (f32[66,8,128]{2,1,0:T(8,128)S(1)}, f32[66,8,128]{2,1,0:T(8,128)S(1)}, u32[]{:S(2)}, u32[]{:S(2)}) collective-permute-start(f32[66,8,128]{2,1,0:T(8,128)S(1)} %get-tuple-element.85), channel_id=1, source_target_pairs={{0,8},{8,0},{16,24},{24,16},{1,9},{9,1},{17,25},{25,17},{2,10},{10... | collective-permute-start | bytes 811016 | tf_op jit(solution)/shard_map/ppermute | solution.py:661
  53.6 5.7 %collective-permute-start.16 = (bf16[66,8,128]{2,1,0:T(8,128)(2,1)S(1)}, bf16[66,8,128]{2,1,0:T(8,128)(2,1)S(1)}, u32[]{:S(2)}, u32[]{:S(2)}) collective-permute-start(bf16[66,8,128]{2,1,0:T(8,128)(2,1)S(1)} %get-tuple-element.105), channel_id=1, source_target_pairs={{0,16},{8,24},{16,0},{24,8},{1,17},{9,25},{17,1},{25,9},{2,18},{10... | collective-permute-start | bytes 405512 | tf_op jit(solution)/shard_map/ppermute | solution.py:661
  59.4 1.4 %collective-permute-start.17 = (bf16[66,8,128]{2,1,0:T(8,128)(2,1)S(1)}, bf16[66,8,128]{2,1,0:T(8,128)(2,1)S(1)}, u32[]{:S(2)}, u32[]{:S(2)}) collective-permute-start(bf16[66,8,128]{2,1,0:T(8,128)(2,1)S(1)} %multiply_convert_fusion.mine_ref), channel_id=1, source_target_pairs={{0,8},{8,0},{16,24},{24,16},{1,9},{9,1},{17,25},{25,17},{2,10},{10... | collective-permute-start | bytes 405512 | tf_op jit(solution)/shard_map/ppermute | solution.py:661
  63.9 1.6 %collective-permute-start.18 = (f32[64,8,128]{2,1,0:T(8,128)S(1)}, f32[64,8,128]{2,1,0:T(8,128)S(1)}, u32[]{:S(2)}, u32[]{:S(2)}) collective-permute-start(f32[64,8,128]{2,1,0:T(8,128)S(1)} %get-tuple-element.92), channel_id=1, source_target_pairs={{0,8},{8,0},{16,24},{24,16},{1,9},{9,1},{17,25},{25,17},{2,10},{10... | collective-permute-start | bytes 786440 | tf_op jit(solution)/shard_map/ppermute | solution.py:661
  65.6 5.6 %collective-permute-start.19 = (f32[64,4,128]{2,1,0:T(4,128)S(1)}, f32[64,4,128]{2,1,0:T(4,128)S(1)}, u32[]{:S(2)}, u32[]{:S(2)}) collective-permute-start(f32[64,4,128]{2,1,0:T(4,128)S(1)} %get-tuple-element.94), channel_id=1, source_target_pairs={{0,16},{8,24},{16,0},{24,8},{1,17},{9,25},{17,1},{25,9},{2,18},{10... | collective-permute-start | bytes 393224 | tf_op jit(solution)/shard_map/ppermute | solution.py:661
